TPU v7x, 256 devices: a whole 4x4x8 slice. The times are simulated.
256 devices in a mesh: dp: 16 (over z_hi, y, core), expert: 16 (over x, z_lo).
Axes of the slice: x: 4, y: 4, z: 8 (z_hi: 2, z_lo: 4; z = z_hi * 4 + z_lo), core: 2. Of those that a mesh axis runs over, the one named last changes fastest.
Arguments:
- layer_inputs: bfloat16 [32768, 2560], P(('dp', 'expert')), may hold values from -6 to 6
- cotangent: bfloat16 [32768, 2560], P(('dp', 'expert')), may hold values from -3 to 3
- expert_ids: int32 [32768, 3], P(('dp', 'expert')), may hold values from 0 to 15, all different within a row; in each aligned block of 128 rows (0 to 127, 128 to 255, ...) at most 26 rows name the same one
- route_weights: bfloat16 [32768, 3], P(('dp', 'expert')), may hold values from 0.049804688 to 0.59765625
- w_gate_up: bfloat16 [16, 2560, 1536], P('expert'), may hold values from -0.125 to 0.125
- w_down: bfloat16 [16, 768, 2560], P('expert', None, 'dp'), may hold values from -0.21875 to 0.21875
Outputs:
- input_grad: bfloat16 [32768, 2560], P(('dp', 'expert'))
- gate_grad: bfloat16 [32768, 3], P(('dp', 'expert'))
- grad_gate_up: bfloat16 [16, 2560, 1536], P('expert', 'dp')
- grad_down: bfloat16 [16, 768, 2560], P('expert', None, 'dp')
Inputs may be any that keep to these rules, and one draw needn't show every extreme that they name: `expert_ids`: each row names 3 different experts; among the rows of one device no expert is named by more than 26 rows.
All inputs are finite; a program needn't handle non-finite values.
Results may differ from a plain program's by a relative error of at most 0.019.
Values may be sent and summed in bfloat16 or wider, within the bound.
No kernel may reach another device: no remote copies, remote signals or barrier semaphores. Data moves between devices by JAX's collectives and lax.ppermute only.
A program may use at most 128 MiB of HBM per device.

v0:
```python
import functools

import jax
import jax.numpy as jnp
import numpy as np
from jax import lax
from jax.experimental import pallas as pl
from jax.experimental.pallas import tpu as pltpu
from jax.sharding import Mesh
from jax.sharding import PartitionSpec as P

AXES = ("zh", "y", "c", "x", "zl")
SIZES = (2, 4, 2, 4, 4)
CAP = 26
BLOCK = 4 * CAP
SLOTS = 16 * CAP
BF = jnp.bfloat16
F32 = jnp.float32
PLACE = {(2, 0): 0, (1, 1): 1, (2, 1): 2, (3, 0): 3, (1, 0): 4, (3, 1): 5, (0, 0): 6, (0, 1): 7}


def pairs_of(move):
    out = []
    for i in range(int(np.prod(SIZES))):
        zh, y, c, x, zl = (int(v) for v in np.unravel_index(i, SIZES))
        z, y, c, x = move(zh * 4 + zl, y, c, x)
        z, y, c, x = z % 8, y % 4, c % 2, x % 4
        out.append((i, int(np.ravel_multi_index((z // 4, y, c, x, z % 4), SIZES))))
    return out


def shift(dz=0, dy=0, dc=0, dx=0):
    return pairs_of(lambda z, y, c, x: (z + dz, y + dy, c + dc, x + dx))


def z_window(d):
    if d == 2:
        return pairs_of(lambda z, y, c, x: (z + 2 - 4 * (z % 2), y, c, x))
    return shift(dz=1 if d == 1 else -1)


def back(pairs):
    return [(b, a) for a, b in pairs]


def send(v, pairs):
    return lax.ppermute(v, AXES, pairs)


def expert_at(pos, d, dx):
    return lax.rem(pos[0] + dx, 4) * 4 + lax.rem(pos[1] + d, 4)


def prep_kernel(pos, ids, w, xin, cot, *refs):
    rows, ogs, sel_out = refs[:4], refs[4:8], refs[8]
    rank_s, wt_s, s1, s2, sw2 = refs[9:]
    tok = ids.shape[1]
    eid = lax.broadcasted_iota(jnp.int32, (16, tok), 0)
    member = jnp.zeros((16, tok), F32)
    weight = jnp.zeros((16, tok), F32)
    for k in range(3):
        hit = eid == ids[k : k + 1, :]
        member = member + jnp.where(hit, 1.0, 0.0)
        weight = weight + jnp.where(hit, w[k : k + 1, :].astype(F32), 0.0)
    before = jnp.where(
        lax.broadcasted_iota(jnp.int32, (tok, tok), 0)
        < lax.broadcasted_iota(jnp.int32, (tok, tok), 1),
        1.0,
        0.0,
    )
    rank = jnp.dot(member.astype(BF), before.astype(BF), preferred_element_type=F32)
    rank_s[...] = jnp.where(member > 0.0, rank + 1.0, 0.0)
    wt_s[...] = weight
    nth = lax.broadcasted_iota(jnp.int32, (CAP, tok), 0).astype(F32) + 1.0
    for d in range(4):
        for dx in range(4):
            e = expert_at(pos, d, dx)
            hit = nth == rank_s[pl.ds(e, 1), :]
            one = jnp.where(hit, 1.0, 0.0)
            s1[pl.ds((d * 4 + dx) * CAP, CAP), :] = one
            s2[pl.ds((dx * 4 + d) * CAP, CAP), :] = one
            sw2[pl.ds((dx * 4 + d) * CAP, CAP), :] = jnp.where(hit, wt_s[pl.ds(e, 1), :], 0.0)
    sel1 = s1[...].astype(BF)
    sel_out[...] = s2[...].astype(BF)
    xv = jnp.dot(sel1, xin[...], preferred_element_type=F32).astype(BF)
    cv = jnp.dot(sw2[...].astype(BF), cot[...], preferred_element_type=F32).astype(BF)
    for i in range(4):
        rows[i][...] = xv[i * BLOCK : (i + 1) * BLOCK, :]
        ogs[i][...] = cv[i * BLOCK : (i + 1) * BLOCK, :]


SMEM = pl.BlockSpec(memory_space=pltpu.SMEM)
VMEM = pl.BlockSpec(memory_space=pltpu.VMEM)


def params(mib=16):
    return pltpu.CompilerParams(vmem_limit_bytes=mib * 1024 * 1024)


def call(kernel, args, in_specs, out_shape, out_specs, deps=(), **kw):
    n, m = len(args), len(deps)

    def body(*refs):
        kernel(*refs[:n], *refs[n + m :])

    specs = list(in_specs) + [pl.BlockSpec(memory_space=pl.ANY)] * m
    kw.setdefault("compiler_params", params())
    return pl.pallas_call(body, out_shape=out_shape, in_specs=specs, out_specs=out_specs, **kw)(
        *args, *deps
    )


def cost(flops, nbytes):
    return pl.CostEstimate(flops=int(flops) // 64, bytes_accessed=int(nbytes) // 64, transcendentals=0)


def prep(pos, ids_t, w_t, xin, cot, deps):
    tok, feat = xin.shape
    blk = jax.ShapeDtypeStruct((BLOCK, feat), BF)
    sel = jax.ShapeDtypeStruct((SLOTS, tok), BF)
    return call(
        prep_kernel,
        (pos, ids_t, w_t, xin, cot),
        [SMEM, VMEM, VMEM, VMEM, VMEM],
        [blk] * 8 + [sel],
        [VMEM] * 9,
        deps,
        scratch_shapes=[pltpu.VMEM((16, tok), F32)] * 2 + [pltpu.VMEM((SLOTS, tok), F32)] * 3,
        compiler_params=params(28),
        cost_estimate=cost(4 * SLOTS * tok * feat, 4 * SLOTS * feat + 4 * tok * feat),
        name="prep",
    )


def regroup_values(vals, j):
    return jnp.concatenate([v[j * CAP : (j + 1) * CAP, :] for v in vals], axis=0)


def regroup_kernel(*refs):
    vals = [r[...] for r in refs[:4]]
    for j in range(4):
        refs[4 + j][...] = regroup_values(vals, j)


def regroup(blocks, tile, deps=()):
    width = blocks[0].shape[1]
    spec = pl.BlockSpec((BLOCK, tile), lambda i: (0, i))
    return call(
        regroup_kernel,
        blocks,
        [spec] * 4,
        [jax.ShapeDtypeStruct((BLOCK, width), BF)] * 4,
        [spec] * 4,
        deps,
        grid=(width // tile,),
        cost_estimate=cost(0, 4 * SLOTS * width),
        name="regroup",
    )


def copies_kernel(v, out):
    for k in range(4):
        out[k] = v[...]


def four_copies(v, deps):
    return call(
        copies_kernel,
        (v,),
        [VMEM],
        jax.ShapeDtypeStruct((4,) + v.shape, BF),
        VMEM,
        deps,
        cost_estimate=cost(0, 10 * v.size),
        name="four_copies",
    )


def stack_kernel(pos, *refs):
    vals = [r[...] for r in refs[:4]]
    for j in range(4):
        refs[4][lax.rem(pos[0] - j + 4, 4)] = regroup_values(vals, j)


def regroup_stacked(pos, blocks, tile, deps):
    width = blocks[0].shape[1]
    return call(
        stack_kernel,
        (pos, *blocks),
        [SMEM] + [pl.BlockSpec((BLOCK, tile), lambda i: (0, i))] * 4,
        jax.ShapeDtypeStruct((4, BLOCK, width), BF),
        pl.BlockSpec((4, BLOCK, tile), lambda i: (0, 0, i)),
        deps,
        grid=(width // tile,),
        cost_estimate=cost(0, 4 * SLOTS * width),
        name="regroup",
    )


def assemble_kernel(*refs):
    x_out, og_out = refs[8], refs[9]
    x_out[...] = jnp.concatenate([r[...] for r in refs[:4]], axis=0)
    vals = [r[...] for r in refs[4:8]]
    og_out[...] = jnp.concatenate([regroup_values(vals, j) for j in range(4)], axis=0)


def assemble(xs, ogs, deps):
    width = xs[0].shape[1]
    tile = 512
    spec = pl.BlockSpec((BLOCK, tile), lambda i: (0, i))
    out = pl.BlockSpec((SLOTS, tile), lambda i: (0, i))
    return call(
        assemble_kernel,
        (*xs, *ogs),
        [spec] * 8,
        [jax.ShapeDtypeStruct((SLOTS, width), BF)] * 2,
        [out] * 2,
        deps,
        grid=(width // tile,),
        cost_estimate=cost(0, 8 * SLOTS * width),
        name="assemble",
    )


def hold(v, deps):
    anys = pl.BlockSpec(memory_space=pl.ANY)
    return call(
        lambda v_ref, out_ref: None,
        (v,),
        [anys],
        jax.ShapeDtypeStruct(v.shape, v.dtype),
        anys,
        deps,
        input_output_aliases={0: 0},
        name="hold",
    )


def up_kernel(x, wg, wu, hidden, ca, cb):
    xv = x[...]
    gate = jnp.dot(xv, wg[0], preferred_element_type=F32)
    up = jnp.dot(xv, wu[0], preferred_element_type=F32)
    s = jax.nn.sigmoid(gate)
    silu = gate * s
    hidden[...] = (silu * up).astype(BF)
    ca[...] = up * s * (1.0 + gate * (1.0 - s))
    cb[...] = silu


def up_part(x, w):
    slots, feat = x.shape
    hid = w.shape[2] // 2
    tile = 256
    steps = hid // tile
    out = pl.BlockSpec((slots, tile), lambda i: (0, i))
    return pl.pallas_call(
        up_kernel,
        grid=(steps,),
        out_shape=[
            jax.ShapeDtypeStruct((slots, hid), BF),
            jax.ShapeDtypeStruct((slots, hid), F32),
            jax.ShapeDtypeStruct((slots, hid), F32),
        ],
        in_specs=[
            pl.BlockSpec((slots, feat), lambda i: (0, 0)),
            pl.BlockSpec((1, feat, tile), lambda i: (0, 0, i)),
            pl.BlockSpec((1, feat, tile), lambda i: (0, 0, i + steps)),
        ],
        out_specs=[out] * 3,
        compiler_params=params(46),
        cost_estimate=cost(4 * slots * feat * hid, 4 * feat * hid + 2 * slots * feat),
        name="up_part",
    )(x, w, w)


def down_kernel(part, *refs):
    pos, og, w_own, w_other, hidden, ca, cb = refs[:7]
    pg, pu, dots, wbuf, acc, hv, av, bv, sems = refs[-9:]
    b = pl.program_id(0)
    moves = [
        pltpu.make_async_copy(src, dst, sems.at[k])
        for k, (src, dst) in enumerate(((hidden, hv), (ca, av), (cb, bv)))
    ]

    @pl.when(b == 0)
    def _():
        for m in moves:
            m.start()
        acc[...] = jnp.zeros_like(acc)

    c = pos[4]
    for j in range(2):
        own = pl.multiple_of((2 * j + c) * part, 32)
        other = pl.multiple_of((2 * j + 1 - c) * part, 32)
        wbuf[pl.ds(own, part), :] = w_own[j, 0]
        wbuf[pl.ds(other, part), :] = w_other[j, 0]
    acc[...] += jnp.dot(og[...], wbuf[...], preferred_element_type=F32)

    @pl.when(b == pl.num_programs(0) - 1)
    def _():
        for m in moves:
            m.wait()
        hg = acc[...]
        pg[...] = (hg * av[...]).astype(BF)
        pu[...] = (hg * bv[...]).astype(BF)
        part_dots = jnp.sum(hg * hv[...].astype(F32), axis=1, keepdims=True)
        dots[...] = jnp.broadcast_to(part_dots, dots.shape)


def down_part(pos, og, w_own, w_other, hidden, ca, cb, deps):
    slots, feat = og.shape
    hid = hidden.shape[1]
    part = w_own.shape[2]
    w_spec = pl.BlockSpec(
        (2, 1, part, hid), lambda b, p: (lax.rem(b, 2), lax.div(b, 2), 0, 0)
    )
    anys = pl.BlockSpec(memory_space=pl.ANY)
    whole = lambda *shape: pl.BlockSpec(shape, lambda b, p: (0,) * len(shape))
    return pl.pallas_call(
        functools.partial(down_kernel, part),
        out_shape=[
            jax.ShapeDtypeStruct((slots, hid), BF),
            jax.ShapeDtypeStruct((slots, hid), BF),
            jax.ShapeDtypeStruct((slots, 128), F32),
        ],
        grid_spec=pltpu.PrefetchScalarGridSpec(
            num_scalar_prefetch=1,
            grid=(4,),
            in_specs=[pl.BlockSpec((slots, 4 * part), lambda b, p: (0, b)), w_spec, w_spec]
            + [anys] * (3 + len(deps)),
            out_specs=[whole(slots, hid), whole(slots, hid), whole(slots, 128)],
            scratch_shapes=[
                pltpu.VMEM((4 * part, hid), BF),
                pltpu.VMEM((slots, hid), F32),
                pltpu.VMEM((slots, hid), BF),
                pltpu.VMEM((slots, hid), F32),
                pltpu.VMEM((slots, hid), F32),
                pltpu.SemaphoreType.DMA((3,)),
            ],
        ),
        compiler_params=params(28),
        cost_estimate=cost(2 * slots * feat * hid, 2 * feat * hid + 2 * slots * feat),
        name="down_part",
    )(pos, og, w_own, w_other, hidden, ca, cb, *deps)


CONTRACT_LAST = (((1,), (1,)), ((), ()))
CONTRACT_FIRST = (((0,), (0,)), ((), ()))


def row_kernel(tile, pg, pu, w, dots, *outs):
    i = pl.program_id(0)
    hid = pg.shape[1]
    g = lax.dot_general(pg[...], w[0, :, :hid], CONTRACT_LAST, preferred_element_type=F32)
    g = g + lax.dot_general(pu[...], w[0, :, hid:], CONTRACT_LAST, preferred_element_type=F32)
    g = g.astype(BF)
    at = pl.ds(pl.multiple_of(i * tile, tile), tile)
    vals = [g[j * BLOCK : (j + 1) * BLOCK, :] for j in range(4)]
    for j in range(4):
        outs[j][:, at] = regroup_values(vals, j)

    @pl.when(i == 0)
    def _():
        dv = dots[...]
        hi = dv.astype(BF)
        lo = (dv - hi.astype(F32)).astype(BF)
        lane = lax.broadcasted_iota(jnp.int32, dv.shape, 1)
        both = jnp.where(lane == 0, hi.astype(F32), lo.astype(F32)).astype(BF)
        cols = outs[0].shape[1] - 128
        parts = [both[j * BLOCK : (j + 1) * BLOCK, :] for j in range(4)]
        for j in range(4):
            outs[j][:, cols:] = regroup_values(parts, j)


def row_part(pg, pu, w, dots, deps):
    slots, hid = pg.shape
    feat = w.shape[1]
    tile = 256
    whole = lambda *shape: pl.BlockSpec(shape, lambda i: (0,) * len(shape))
    return call(
        functools.partial(row_kernel, tile),
        (pg, pu, w, dots),
        [
            whole(slots, hid),
            whole(slots, hid),
            pl.BlockSpec((1, tile, 2 * hid), lambda i: (0, i, 0)),
            whole(slots, 128),
        ],
        [jax.ShapeDtypeStruct((BLOCK, feat + 128), BF)] * 4,
        [whole(BLOCK, feat + 128)] * 4,
        deps,
        grid=(feat // tile,),
        compiler_params=params(24),
        cost_estimate=cost(4 * slots * feat * hid, 4 * feat * hid + 6 * slots * hid),
        name="row_part",
    )


def grad_kernel(part, pos, left, *refs):
    rights, mine, other, buf, sems = refs[:-4], refs[-4], refs[-3], refs[-2], refs[-1]
    b = pl.program_id(0)
    slot = lax.rem(b, 2)

    def finish(which):
        for u in range(4):
            pltpu.make_async_copy(buf.at[which, u], mine.at[0], sems.at[which, u]).wait()

    @pl.when(b >= 2)
    def _():
        finish(slot)

    lv = left[...].T
    for k, right in enumerate(rights):
        res = jnp.dot(lv, right[...], preferred_element_type=F32).astype(BF)
        cols = slice(k * res.shape[1], (k + 1) * res.shape[1])
        for u in range(4):
            buf[slot, u, :, cols] = res[u * part : (u + 1) * part, :]

    def out(c):
        for u in range(4):
            to = mine if u % 2 == c else other
            at = pos[5 + b * 2 + u // 2]
            pltpu.make_async_copy(buf.at[slot, u], to.at[at], sems.at[slot, u]).start()

    pl.when(pos[4] == 0)(lambda: out(0))
    pl.when(pos[4] == 1)(lambda: out(1))

    @pl.when(b == pl.num_programs(0) - 1)
    def _():
        finish(1 - slot)
        finish(slot)


def grad_part(pos, left, rights, deps=()):
    slots, feat = left.shape
    cols = sum(r.shape[1] for r in rights)
    part = feat // 16
    return call(
        functools.partial(grad_kernel, part),
        (pos, left, *rights),
        [SMEM, pl.BlockSpec((slots, 4 * part), lambda i: (0, i))]
        + [pl.BlockSpec(r.shape, lambda i: (0, 0)) for r in rights],
        [jax.ShapeDtypeStruct((8, part, cols), BF)] * 2,
        [pl.BlockSpec(memory_space=pl.ANY)] * 2,
        deps,
        grid=(4,),
        scratch_shapes=[pltpu.VMEM((2, 4, part, cols), BF), pltpu.SemaphoreType.DMA((2, 4))],
        compiler_params=params(24),
        cost_estimate=cost(2 * slots * feat * cols, 2 * feat * cols + 2 * slots * feat),
        name="grad_part",
    )


def plus(*vals):
    return sum(v.astype(F32) for v in vals)


def first_kernel(mine, got, up, down):
    total = plus(mine[...], got[...]).astype(BF)
    up[...] = total[:2]
    down[...] = total[2:]


def second_kernel(mine, got, up1, dn1, up, down):
    total = plus(mine[...], got[...])
    up[...] = plus(total[0], up1[0]).astype(BF)
    down[...] = plus(total[1], dn1[0]).astype(BF)


def far_kernel(mine, got, up1, dn1, up2, dn2, out, kept):
    out[...] = plus(mine[1], got[1], up1[0], dn2[...]).astype(BF)
    kept[...] = plus(mine[0], got[0], dn1[0], up2[...])


def last_kernel(kept, far, out):
    out[...] = plus(kept[...], far[...]).astype(BF)


def pieces(shape, count, at, tile):
    return pl.BlockSpec((count,) + shape[1:-1] + (tile,), lambda i: (at, 0, i))


def sums(kernel, args, specs, outs, deps, name):
    tile = 384
    cols = args[0].shape[-1]
    flat = pl.BlockSpec((args[0].shape[-2], tile), lambda i: (0, i))
    nbytes = sum(2 * (sp[0] if sp else 1) * args[0].shape[-2] * cols for sp in specs)
    return call(
        kernel,
        args,
        [flat if sp is None else pieces(a.shape, sp[0], sp[1], tile) for a, sp in zip(args, specs)],
        outs,
        [flat if len(o.shape) == 2 else pieces(o.shape, o.shape[0], 0, tile) for o in outs],
        deps,
        grid=(cols // tile,),
        cost_estimate=cost(0, 2 * nbytes),
        name=name,
    )


def shape_of(a, count=None):
    return jax.ShapeDtypeStruct(((count,) if count else ()) + a.shape[1:], BF)


def first_sum(mine, got, deps):
    args, outs = (mine, got), [shape_of(mine, 2)] * 2
    up, down = sums(first_kernel, args, [(4, 0)] * 2, outs, deps, "first_sum")
    return send(up, shift(dy=1)), send(down, shift(dy=-1)), [up]


def second_sum(mine, got, up1, dn1, deps):
    args, outs = (mine, got, up1, dn1), [shape_of(mine)] * 2
    specs = [(2, 2), (2, 2), (1, 0), (1, 0)]
    up, down = sums(second_kernel, args, specs, outs, deps, "second_sum")
    return send(up, shift(dy=1)), send(down, shift(dy=-1)), [up]


def far_sum(mine, got, up1, dn1, up2, dn2, deps):
    args = (mine, got, up1, dn1, up2, dn2)
    outs = [shape_of(mine), jax.ShapeDtypeStruct(mine.shape[1:], F32)]
    specs = [(2, 3), (2, 3), (1, 1), (1, 1), None, None]
    out, kept = sums(far_kernel, args, specs, outs, deps, "far_sum")
    return send(out, shift(dz=4)), kept, [out]


def last_sum(kept, far, deps):
    (out,) = sums(last_kernel, (kept, far), [None] * 2, [shape_of(kept[None])], deps, "last_sum")
    return out


def final_kernel(pos, ids, w, sel, back, grad, gate):
    feat = grad.shape[1]
    acc = jnp.zeros(grad.shape, F32)
    sv = sel[...].astype(F32)
    gates = [jnp.zeros((1, grad.shape[0]), F32) for _ in range(3)]
    for j in range(4):
        at = lax.rem(pos[0] + j, 4)
        part = sv[j * BLOCK : (j + 1) * BLOCK, :]
        acc += lax.dot_general(
            part.astype(BF), back[at, :, :feat], CONTRACT_FIRST, preferred_element_type=F32
        )
        tail = back[at, :, feat:].astype(F32)
        found = part * (tail[:, 0:1] + tail[:, 1:2])
        for d in range(4):
            val = jnp.sum(found[d * CAP : (d + 1) * CAP, :], axis=0, keepdims=True)
            e = expert_at(pos, d, j)
            for k in range(3):
                gates[k] += jnp.where(ids[k : k + 1, :] == e, val, 0.0)
    grad[...] = acc.astype(BF)
    for k in range(3):
        gate[k : k + 1, :] = (gates[k] / w[k : k + 1, :].astype(F32)).astype(BF)


def final(pos, ids_t, w_t, sel, back, feat, deps):
    tok = ids_t.shape[1]
    return call(
        final_kernel,
        (pos, ids_t, w_t, sel, back),
        [SMEM] + [VMEM] * 4,
        [jax.ShapeDtypeStruct((tok, feat), BF), jax.ShapeDtypeStruct((3, tok), BF)],
        [VMEM] * 2,
        deps,
        cost_estimate=cost(2 * SLOTS * tok * feat, 2 * SLOTS * feat + 2 * tok * feat),
        name="final",
    )


def on_device(layer_inputs, cotangent, expert_ids, route_weights, w_gate_up, w_down):
    feat = layer_inputs.shape[1]
    zh, y, c, x, zl = (lax.axis_index(a) for a in AXES)
    places = jnp.zeros((8,), jnp.int32)
    unit = jnp.arange(8, dtype=jnp.int32)
    rel = ((unit % 4 - y) % 4) * 2 + (unit // 4 + zh) % 2
    for (dy, dzh), at in PLACE.items():
        places = jnp.where(rel == dy * 2 + dzh, at, places)
    pos = jnp.concatenate([jnp.stack([x, zl, zh, y, c]).astype(jnp.int32), places])
    ids_t, w_t = expert_ids.T, route_weights.T

    wd = w_down[0].T
    wd_two = jnp.stack([wd, wd])
    wd_zh = lax.all_to_all(wd_two, "zh", 0, 0, tiled=True)
    made = prep(pos, ids_t, w_t, layer_inputs, cotangent, [wd_two])
    rows, ogs, sel = made[:4], made[4:8], made[8]
    z_moves = [z_window(d) for d in (1, 2, 3)]
    x_moves = [shift(dx=d) for d in (1, 2, 3)]
    over = lambda blocks, moves: [blocks[0]] + [send(b, m) for b, m in zip(blocks[1:], moves)]
    home = lambda blocks, moves: over(blocks, [back(m) for m in moves])
    flip = lambda v: send(v, shift(dc=1))
    rows = over(rows, z_moves)
    pairs = four_copies(wd_zh, [rows[1]])
    rows = regroup(rows, 512, [pairs])
    wd_own = lax.all_to_all(pairs, "y", 0, 0, tiled=True)
    ogs = regroup(over(ogs, x_moves), 512, [rows[0]])
    xs, og = assemble(over(rows, x_moves), over(ogs, z_moves), [])
    wd_own = hold(wd_own, [xs])
    wd_other = flip(wd_own)

    hidden, ca, cb = up_part(xs, w_gate_up)
    pg, pu, dots = down_part(pos, og, wd_own, wd_other, hidden, ca, cb, [])
    g_own, other = grad_part(pos, xs, [pg, pu])
    g_got = flip(other)
    d_own, other = grad_part(pos, og, [hidden], [g_own])
    d_got = flip(other)
    g_up1, g_dn1, dep = first_sum(g_own, g_got, [d_own])
    d_up1, d_dn1, dep = first_sum(d_own, d_got, dep)
    row_grads = row_part(pg, pu, w_gate_up, dots, dep)
    g_up2, g_dn2, dep = second_sum(g_own, g_got, g_up1, g_dn1, [row_grads[0]])
    g_far, g_kept, dep = far_sum(g_own, g_got, g_up1, g_dn1, g_up2, g_dn2, dep)
    back_rows = regroup_stacked(pos, home(row_grads, z_moves), (feat + 128) // 3, dep)
    back_rows_x = lax.all_to_all(back_rows, "x", 0, 0, tiled=True)
    d_up2, d_dn2, dep = second_sum(d_own, d_got, d_up1, d_dn1, [back_rows])
    gu_grad = last_sum(g_kept, g_far, dep)
    d_far, d_kept, dep = far_sum(d_own, d_got, d_up1, d_dn1, d_up2, d_dn2, [gu_grad])
    input_grad, gate_grad = final(pos, ids_t, w_t, sel, back_rows_x, feat, dep)
    down_grad = last_sum(d_kept, d_far, [input_grad])
    return (input_grad, gate_grad.T, gu_grad[None], down_grad.T[None])


def solution(mesh):
    grid = Mesh(mesh.devices.reshape(SIZES), AXES)
    dp, ex = AXES[:3], AXES[3:]
    return jax.shard_map(
        on_device,
        mesh=grid,
        in_specs=(
            P(AXES, None),
            P(AXES, None),
            P(AXES, None),
            P(AXES, None),
            P(ex, None, None),
            P(ex, None, dp),
        ),
        out_specs=(
            P(AXES, None),
            P(AXES, None),
            P(ex, dp, None),
            P(ex, None, dp),
        ),
        check_vma=False,
    )
```

profile of v0, /device:TPU:6, one launch (start us, length us, event | category | flops | bytes accessed | tf_op | source)
XLA Modules:
  0.0 233.4 jit_solution(3343600288592680739)
XLA Ops:
  0.6 1.9 pad_maximum_fusion.refs_5_
  2.7 1.1 copy-done.9
  3.8 1.1 copy-done.10
  4.8 0.7 copy-done.14
  6.2 3.0 %prep.1 = (bf16[104,2560]{1,0:T(8,128)(2,1)S(1)}, bf16[104,2560]{1,0:T(8,128)(2,1)S(1)}, bf16[104,2560]{1,0:T(8,128)(2,1)}, bf16[104,2560]{1,0:T(8,128)(2,1)}, b...) custom-call(s32[13]{0:T(128)S(1)} %concatenate.3.refs_0_, ...), custom_call_target="tpu_custom_call" | custom-call | flops 8519680 | bytes 87040 | tf_op jit(solution)/shard_map/prep/pallas_call | solution.py:108
  9.2 0.8 copy-done.11
  10.0 0.8 copy-done.18
  10.9 1.9 collective-permute-start
  12.8 7.6 %all-to-all-start = ((bf16[2,160,768]{2,1,0:T(8,128)(2,1)}), bf16[2,160,768]{2,1,0:T(8,128)(2,1)S(1)}, u32[]{:S(2)}, u32[]{:S(2)}) async-start(bf16[2,160,768]{2,1,0:T(8,128)(2,1)} %pad_maximum_fusion.refs_5_), calls=%async_computation | async-start | bytes 983040 | tf_op jit(solution)/shard_map/all_to_all | solution.py:581
  20.3 1.5 collective-permute-start.1
  21.8 4.6 %collective-permute-start.2 = (bf16[104,2560]{1,0:T(8,128)(2,1)}, bf16[104,2560]{1,0:T(8,128)(2,1)}, u32[]{:S(2)}, u32[]{:S(2)}) collective-permute-start(bf16[104,2560]{1,0:T(8,128)(2,1)} %get-tuple-element.55), channel_id=1, source_target_pairs={{0,131},{1,0},{2,1},{3,2},{4,135},{5,4},{6,5},{7,6},{8,139},{9,8},... | collective-permute-start | bytes 1597448 | tf_op jit(solution)/shard_map/ppermute | solution.py:47
  26.9 2.4 %collective-permute-start.7 = (bf16[104,2560]{1,0:T(8,128)(2,1)}, bf16[104,2560]{1,0:T(8,128)(2,1)S(1)}, u32[]{:S(2)}, u32[]{:S(2)}) collective-permute-start(bf16[104,2560]{1,0:T(8,128)(2,1)} %get-tuple-element.62), channel_id=1, source_target_pairs={{0,8},{1,9},{2,10},{3,11},{4,12},{5,13},{6,14},{7,15},{8,0},{9,1},... | collective-permute-start | bytes 1597448 | tf_op jit(solution)/shard_map/ppermute | solution.py:47
  29.6 12.9 %all-to-all-done.refs_0_ = bf16[2,160,768]{2,1,0:T(8,128)(2,1)S(1)} async-done(((bf16[2,160,768]{2,1,0:T(8,128)(2,1)}), bf16[2,160,768]{2,1,0:T(8,128)(2,1)S(1)}, u32[]{:S(2)}, u32[]{:S(2)}) %all-to-all-start) | async-done | bytes 491552 | tf_op jit(solution)/shard_map/all_to_all | solution.py:581
  42.5 1.4 four_copies.1.refs_4_
  44.0 4.5 %all-to-all-start.1 = ((bf16[4,2,160,768]{3,2,1,0:T(8,128)(2,1)}), bf16[4,2,160,768]{3,2,1,0:T(8,128)(2,1)}, u32[]{:S(2)}, u32[]{:S(2)}) async-start(bf16[4,2,160,768]{3,2,1,0:T(8,128)(2,1)} %four_copies.1.refs_4_), calls=%async_computation.1 | async-start | bytes 3932160 | tf_op jit(solution)/shard_map/all_to_all | solution.py:592
  48.4 3.6 %collective-permute-done.1.refs_2_ = bf16[104,2560]{1,0:T(8,128)(2,1)} collective-permute-done((bf16[104,2560]{1,0:T(8,128)(2,1)}, bf16[104,2560]{1,0:T(8,128)(2,1)}, u32[]{:S(2)}, u32[]{:S(2)}) %collective-permute-start.1) | collective-permute-done | bytes 532512 | tf_op jit(solution)/shard_map/ppermute | solution.py:47
  52.0 3.1 %collective-permute-done.2.refs_3_ = bf16[104,2560]{1,0:T(8,128)(2,1)} collective-permute-done((bf16[104,2560]{1,0:T(8,128)(2,1)}, bf16[104,2560]{1,0:T(8,128)(2,1)}, u32[]{:S(2)}, u32[]{:S(2)}) %collective-permute-start.2) | collective-permute-done | bytes 532512 | tf_op jit(solution)/shard_map/ppermute | solution.py:47
  55.2 1.0 copy-done.12
  56.2 3.2 %regroup.3 = (bf16[104,2560]{1,0:T(8,128)(2,1)S(1)}, bf16[104,2560]{1,0:T(8,128)(2,1)S(1)}, bf16[104,2560]{1,0:T(8,128)(2,1)S(1)}, bf16[104,2560]{1,0:T(8,128)(2,1)S(1)}) custom-call(bf16[104,2560]{1,0:T(8,128)(2,1)S(1)} %copy-done.12, bf16[104,2560]{1,0:T(8,128)(2,1)S(1)} %collective-permute-done.refs_1_, bf16[104,2560]{1,0:T(8,128)(2,1)} %collective-permute-done.1.refs_2_, ...), custom_call_target="tpu_custom_call" | custom-call | bytes 66560 | tf_op jit(solution)/shard_map/regroup/pallas_call | solution.py:108
  59.5 0.7 regroup.4
  60.2 1.7 collective-permute-start.9
  61.9 5.6 %collective-permute-start.10 = (bf16[104,2560]{1,0:T(8,128)(2,1)S(1)}, bf16[104,2560]{1,0:T(8,128)(2,1)S(1)}, u32[]{:S(2)}, u32[]{:S(2)}) collective-permute-start(bf16[104,2560]{1,0:T(8,128)(2,1)S(1)} %get-tuple-element.66), channel_id=1, source_target_pairs={{0,2},{1,131},{2,128},{3,1},{4,6},{5,135},{6,132},{7,5},{8,10},{9,... | collective-permute-start | bytes 1597448 | tf_op jit(solution)/shard_map/ppermute | solution.py:47
  67.5 1.8 collective-permute-start.4
  69.4 5.8 %collective-permute-done.9.refs_5_ = bf16[104,2560]{1,0:T(8,128)(2,1)S(1)} collective-permute-done((bf16[104,2560]{1,0:T(8,128)(2,1)S(1)}, bf16[104,2560]{1,0:T(8,128)(2,1)S(1)}, u32[]{:S(2)}, u32[]{:S(2)}) %collective-permute-start.9) | collective-permute-done | bytes 532512 | tf_op jit(solution)/shard_map/ppermute | solution.py:47
  75.2 0.8 collective-permute-start.5
  76.0 11.8 %collective-permute-done.10.refs_6_ = bf16[104,2560]{1,0:T(8,128)(2,1)S(1)} collective-permute-done((bf16[104,2560]{1,0:T(8,128)(2,1)S(1)}, bf16[104,2560]{1,0:T(8,128)(2,1)S(1)}, u32[]{:S(2)}, u32[]{:S(2)}) %collective-permute-start.10) | collective-permute-done | bytes 532512 | tf_op jit(solution)/shard_map/ppermute | solution.py:47
  87.9 5.1 %collective-permute-done.5.refs_3_ = bf16[104,2560]{1,0:T(8,128)(2,1)S(1)} collective-permute-done((bf16[104,2560]{1,0:T(8,128)(2,1)S(1)}, bf16[104,2560]{1,0:T(8,128)(2,1)S(1)}, u32[]{:S(2)}, u32[]{:S(2)}) %collective-permute-start.5) | collective-permute-done | bytes 532512 | tf_op jit(solution)/shard_map/ppermute | solution.py:47
  93.0 1.2 assemble.1
  94.3 1.4 copy-done.5
  95.7 6.4 %up_part.1 = (bf16[416,768]{1,0:T(8,128)(2,1)S(1)}, f32[416,768]{1,0:T(8,128)S(1)}, f32[416,768]{1,0:T(8,128)S(1)}) custom-call(bf16[416,2560]{1,0:T(8,128)(2,1)S(1)} %get-tuple-element.69.refs_1_.x, bf16[1,2560,1536]{2,1,0:T(8,128)(2,1)} %refs_2_.1, bf16[1,2560,1536]{2,1,0:T(8,128)(2,1)} %refs_2_.1), custom_call_target="tpu_custom_call" | custom-call | flops 51118080 | bytes 156160 | tf_op jit(solution)/shard_map/up_part/pallas_call | solution.py:256
  102.2 6.5 %down_part.1 = (bf16[416,768]{1,0:T(8,128)(2,1)S(1)}, bf16[416,768]{1,0:T(8,128)(2,1)S(1)}, f32[416,128]{1,0:T(8,128)S(1)}) custom-call(s32[13]{0:T(128)S(1)} %concatenate.3.refs_0_, bf16[416,2560]{1,0:T(8,128)(2,1)S(1)} %copy-done.6, bf16[4,2,160,768]{3,2,1,0:T(8,128)(2,1)} %hold.1.refs_2_, bf16[4,2,160,768]{3,2,1,0:T(8,128)(2,1)S(1)} %collective-permute-done.12.refs_3_, ...), custom_call_target="tpu_custom_call" | custom-call | flops 25559040 | bytes 94720 | tf_op jit(solution)/shard_map/down_part/pallas_call | solution.py:319
  108.6 10.9 %grad_part.2 = (bf16[8,160,1536]{2,1,0:T(8,128)(2,1)S(1)}, bf16[8,160,1536]{2,1,0:T(8,128)(2,1)S(1)}) custom-call(s32[13]{0:T(128)S(1)} %concatenate.3.refs_0_, bf16[416,2560]{1,0:T(8,128)(2,1)S(1)} %get-tuple-element.69.refs_1_.x, bf16[416,768]{1,0:T(8,128)(2,1)S(1)} %get-tuple-element.73.refs_2_.refs_0_, bf16[416,768]{1,0:T(8,128)(2,1)S(1)} %get-tuple-element.74.refs_3_.refs_1_), custom_call_target="tpu_custom_call" | custom-call | flops 51118080 | bytes 156160 | tf_op jit(solution)/shard_map/grad_part/pallas_call | solution.py:108
  119.9 9.0 %grad_part.3 = (bf16[8,160,768]{2,1,0:T(8,128)(2,1)S(1)}, bf16[8,160,768]{2,1,0:T(8,128)(2,1)S(1)}) custom-call(s32[13]{0:T(128)S(1)} %concatenate.3.refs_0_, bf16[416,2560]{1,0:T(8,128)(2,1)S(1)} %copy-done.6, bf16[416,768]{1,0:T(8,128)(2,1)S(1)} %get-tuple-element.70.refs_4_.refs_2_, bf16[8,160,1536]{2,1,0:T(8,128)(2,1)S(1)} %get-tuple-element.76.refs_3_.refs_0_), custom_call_target="tpu_custom_call" | custom-call | flops 25559040 | bytes 94720 | tf_op jit(solution)/shard_map/grad_part/pallas_call | solution.py:108
  129.2 1.1 first_sum.2
  130.3 3.1 %collective-permute-start.19 = (bf16[2,160,1536]{2,1,0:T(8,128)(2,1)S(1)}, bf16[2,160,1536]{2,1,0:T(8,128)(2,1)S(1)}, u32[]{:S(2)}, u32[]{:S(2)}) collective-permute-start(bf16[2,160,1536]{2,1,0:T(8,128)(2,1)S(1)} %get-tuple-element.86), channel_id=1, source_target_pairs={{0,96},{1,97},{2,98},{3,99},{4,100},{5,101},{6,102},{7,103},{8,104... | collective-permute-start | bytes 2949128 | tf_op jit(solution)/shard_map/ppermute | solution.py:47
  134.1 0.7 copy-done.2
  134.7 0.8 copy-done.19
  135.5 5.5 %row_part.1 = (bf16[104,2688]{1,0:T(8,128)(2,1)S(1)}, bf16[104,2688]{1,0:T(8,128)(2,1)S(1)}, bf16[104,2688]{1,0:T(8,128)(2,1)S(1)}, bf16[104,2688]{1,0:T(8,128)(2,1)S(1)}) custom-call(bf16[416,768]{1,0:T(8,128)(2,1)S(1)} %get-tuple-element.73.refs_2_.refs_0_, bf16[416,768]{1,0:T(8,128)(2,1)S(1)} %get-tuple-element.74.refs_3_.refs_1_, ...), custom_call_target="tpu_custom_call" | custom-call | flops 51118080 | bytes 152832 | tf_op jit(solution)/shard_map/row_part/pallas_call | solution.py:108
  141.3 5.3 %collective-permute-start.16 = (bf16[104,2688]{1,0:T(8,128)(2,1)S(1)}, bf16[104,2688]{1,0:T(8,128)(2,1)S(1)}, u32[]{:S(2)}, u32[]{:S(2)}) collective-permute-start(bf16[104,2688]{1,0:T(8,128)(2,1)S(1)} %get-tuple-element.84), channel_id=1, source_target_pairs={{2,0},{131,1},{128,2},{1,3},{6,4},{135,5},{132,6},{5,7},{10,8},{13... | collective-permute-start | bytes 1677320 | tf_op jit(solution)/shard_map/ppermute | solution.py:47
  146.6 4.5 %collective-permute-start.17 = (bf16[104,2688]{1,0:T(8,128)(2,1)S(1)}, bf16[104,2688]{1,0:T(8,128)(2,1)S(1)}, u32[]{:S(2)}, u32[]{:S(2)}) collective-permute-start(bf16[104,2688]{1,0:T(8,128)(2,1)S(1)} %get-tuple-element.85), channel_id=1, source_target_pairs={{131,0},{0,1},{1,2},{2,3},{135,4},{4,5},{5,6},{6,7},{139,8},{8,9},... | collective-permute-start | bytes 1677320 | tf_op jit(solution)/shard_map/ppermute | solution.py:47
  151.1 3.9 %collective-permute-done.19.refs_3_ = bf16[2,160,1536]{2,1,0:T(8,128)(2,1)S(1)} collective-permute-done((bf16[2,160,1536]{2,1,0:T(8,128)(2,1)S(1)}, bf16[2,160,1536]{2,1,0:T(8,128)(2,1)S(1)}, u32[]{:S(2)}, u32[]{:S(2)}) %collective-permute-start.19) | collective-permute-done | bytes 983072 | tf_op jit(solution)/shard_map/ppermute | solution.py:47
  154.9 3.4 %collective-permute-done.18.refs_2_ = bf16[2,160,1536]{2,1,0:T(8,128)(2,1)S(1)} collective-permute-done((bf16[2,160,1536]{2,1,0:T(8,128)(2,1)S(1)}, bf16[2,160,1536]{2,1,0:T(8,128)(2,1)S(1)}, u32[]{:S(2)}, u32[]{:S(2)}) %collective-permute-start.18) | collective-permute-done | bytes 983072 | tf_op jit(solution)/shard_map/ppermute | solution.py:47
  158.3 0.9 second_sum.2
  159.6 1.7 collective-permute-start.20
  161.3 10.3 %collective-permute-done.21.refs_5_ = bf16[160,1536]{1,0:T(8,128)(2,1)S(1)} collective-permute-done((bf16[160,1536]{1,0:T(8,128)(2,1)S(1)}, bf16[160,1536]{1,0:T(8,128)(2,1)S(1)}, u32[]{:S(2)}, u32[]{:S(2)}) %collective-permute-start.21) | collective-permute-done | bytes 491552 | tf_op jit(solution)/shard_map/ppermute | solution.py:47
  171.6 1.5 collective-permute-done.20.refs_4_
  173.1 1.1 far_sum.2
  174.3 1.3 regroup.5.refs_4_
  175.6 1.4 copy-done
  177.0 0.8 copy-done.13
  177.8 5.5 %all-to-all-start.2 = ((bf16[4,104,2688]{2,1,0:T(8,128)(2,1)}), bf16[4,104,2688]{2,1,0:T(8,128)(2,1)}, u32[]{:S(2)}, u32[]{:S(2)}) async-start(bf16[4,104,2688]{2,1,0:T(8,128)(2,1)} %copy-done), calls=%async_computation.2 | async-start | bytes 4472832 | tf_op jit(solution)/shard_map/all_to_all | solution.py:610
  183.6 1.7 collective-permute-start.22
  185.3 11.6 %collective-permute-start.26 = (bf16[160,1536]{1,0:T(8,128)(2,1)}, bf16[160,1536]{1,0:T(8,128)(2,1)S(1)}, u32[]{:S(2)}, u32[]{:S(2)}) collective-permute-start(bf16[160,1536]{1,0:T(8,128)(2,1)} %copy-done.13), channel_id=1, source_target_pairs={{0,128},{1,129},{2,130},{3,131},{4,132},{5,133},{6,134},{7,135},{8... | collective-permute-start | bytes 1474568 | tf_op jit(solution)/shard_map/ppermute | solution.py:47
  196.9 1.6 copy-done.1
  198.5 1.5 copy-done.3
  200.5 1.6 collective-permute-start.25
  202.6 13.6 %collective-permute-done.26.refs_1_ = bf16[160,1536]{1,0:T(8,128)(2,1)S(1)} collective-permute-done((bf16[160,1536]{1,0:T(8,128)(2,1)}, bf16[160,1536]{1,0:T(8,128)(2,1)S(1)}, u32[]{:S(2)}, u32[]{:S(2)}) %collective-permute-start.26) | collective-permute-done | bytes 491552 | tf_op jit(solution)/shard_map/ppermute | solution.py:47
  216.2 1.5 last_sum.2.refs_6_
  217.8 1.0 copy-done.7
  219.4 3.6 %collective-permute-start.27 = (bf16[160,768]{1,0:T(8,128)(2,1)S(1)}, bf16[160,768]{1,0:T(8,128)(2,1)S(1)}, u32[]{:S(2)}, u32[]{:S(2)}) collective-permute-start(bf16[160,768]{1,0:T(8,128)(2,1)S(1)} %get-tuple-element.94.refs_5_), channel_id=1, source_target_pairs={{0,128},{1,129},{2,130},{3,131},{4,132},{5,133},{6,134},{7,135},{8... | collective-permute-start | bytes 737288 | tf_op jit(solution)/shard_map/ppermute | solution.py:47
  223.0 3.3 %final.1 = (bf16[128,2560]{1,0:T(8,128)(2,1)}, bf16[3,128]{1,0:T(4,128)(2,1)}) custom-call(s32[13]{0:T(128)S(1)} %concatenate.3.refs_0_, s32[3,128]{1,0:T(4,128)S(1)} %bitcast.21, bf16[3,128]{1,0:T(4,128)(2,1)S(1)} %bitcast.23, bf16[416,128]{1,0:T(8,128)(2,1)S(1)} %get-tuple-element.51.refs_3_, bf16[4,104,2688]{2,1,0:T(8,128)(2,1)} %all-to-all-done.2.refs_4_, ...), custom_call_target="tpu_custom_call" | custom-call | flops 4259840 | bytes 43520 | tf_op jit(solution)/shard_map/final/pallas_call | solution.py:108
  226.4 5.1 %collective-permute-done.27.refs_1_ = bf16[160,768]{1,0:T(8,128)(2,1)S(1)} collective-permute-done((bf16[160,768]{1,0:T(8,128)(2,1)S(1)}, bf16[160,768]{1,0:T(8,128)(2,1)S(1)}, u32[]{:S(2)}, u32[]{:S(2)}) %collective-permute-start.27) | collective-permute-done | bytes 245792 | tf_op jit(solution)/shard_map/ppermute | solution.py:47
  231.5 1.1 copy-done.8
  232.6 0.8 last_sum.3
  (67 shorter events, 5.6 us)
Async XLA Ops:
  2.7 1.1 copy-start.9
  3.8 1.1 copy-start.10
  4.8 0.7 copy-start.14
  5.5 0.7 copy-start.16
  9.2 0.8 copy-start.11
  10.0 0.8 copy-start.18
  10.9 18.4 %collective-permute-start = (bf16[104,2560]{1,0:T(8,128)(2,1)S(1)}, bf16[104,2560]{1,0:T(8,128)(2,1)S(1)}, u32[]{:S(2)}, u32[]{:S(2)}) collective-permute-start(bf16[104,2560]{1,0:T(8,128)(2,1)S(1)} %get-tuple-element.53), channel_id=1, source_target_pairs={{0,1},{1,2},{2,3},{3,128},{4,5},{5,6},{6,7},{7,132},{8,9},{9,10},{... | collective-permute-start | bytes 1597448 | tf_op jit(solution)/shard_map/ppermute | solution.py:47
  12.8 29.7 %all-to-all-start = ((bf16[2,160,768]{2,1,0:T(8,128)(2,1)}), bf16[2,160,768]{2,1,0:T(8,128)(2,1)S(1)}, u32[]{:S(2)}, u32[]{:S(2)}) async-start(bf16[2,160,768]{2,1,0:T(8,128)(2,1)} %pad_maximum_fusion.refs_5_), calls=%async_computation | async-start | bytes 983040 | tf_op jit(solution)/shard_map/all_to_all | solution.py:581
  20.3 31.7 %collective-permute-start.1 = (bf16[104,2560]{1,0:T(8,128)(2,1)}, bf16[104,2560]{1,0:T(8,128)(2,1)}, u32[]{:S(2)}, u32[]{:S(2)}) collective-permute-start(bf16[104,2560]{1,0:T(8,128)(2,1)} %get-tuple-element.54), channel_id=1, source_target_pairs={{0,2},{1,131},{2,128},{3,1},{4,6},{5,135},{6,132},{7,5},{8,10},{9,... | collective-permute-start | bytes 1597448 | tf_op jit(solution)/shard_map/ppermute | solution.py:47
  21.8 33.4 %collective-permute-start.2 = (bf16[104,2560]{1,0:T(8,128)(2,1)}, bf16[104,2560]{1,0:T(8,128)(2,1)}, u32[]{:S(2)}, u32[]{:S(2)}) collective-permute-start(bf16[104,2560]{1,0:T(8,128)(2,1)} %get-tuple-element.55), channel_id=1, source_target_pairs={{0,131},{1,0},{2,1},{3,2},{4,135},{5,4},{6,5},{7,6},{8,139},{9,8},... | collective-permute-start | bytes 1597448 | tf_op jit(solution)/shard_map/ppermute | solution.py:47
  26.4 33.1 %collective-permute-start.6 = (bf16[104,2560]{1,0:T(8,128)(2,1)}, bf16[104,2560]{1,0:T(8,128)(2,1)S(1)}, u32[]{:S(2)}, u32[]{:S(2)}) collective-permute-start(bf16[104,2560]{1,0:T(8,128)(2,1)} %get-tuple-element.61), channel_id=1, source_target_pairs={{0,4},{1,5},{2,6},{3,7},{4,8},{5,9},{6,10},{7,11},{8,12},{9,13},{1... | collective-permute-start | bytes 1597448 | tf_op jit(solution)/shard_map/ppermute | solution.py:47
  26.9 32.6 %collective-permute-start.7 = (bf16[104,2560]{1,0:T(8,128)(2,1)}, bf16[104,2560]{1,0:T(8,128)(2,1)S(1)}, u32[]{:S(2)}, u32[]{:S(2)}) collective-permute-start(bf16[104,2560]{1,0:T(8,128)(2,1)} %get-tuple-element.62), channel_id=1, source_target_pairs={{0,8},{1,9},{2,10},{3,11},{4,12},{5,13},{6,14},{7,15},{8,0},{9,1},... | collective-permute-start | bytes 1597448 | tf_op jit(solution)/shard_map/ppermute | solution.py:47
  29.3 30.2 %collective-permute-start.8 = (bf16[104,2560]{1,0:T(8,128)(2,1)}, bf16[104,2560]{1,0:T(8,128)(2,1)S(1)}, u32[]{:S(2)}, u32[]{:S(2)}) collective-permute-start(bf16[104,2560]{1,0:T(8,128)(2,1)} %copy-done.18), channel_id=1, source_target_pairs={{0,12},{1,13},{2,14},{3,15},{4,0},{5,1},{6,2},{7,3},{8,4},{9,5},{1... | collective-permute-start | bytes 1597448 | tf_op jit(solution)/shard_map/ppermute | solution.py:47
  44.0 51.7 %all-to-all-start.1 = ((bf16[4,2,160,768]{3,2,1,0:T(8,128)(2,1)}), bf16[4,2,160,768]{3,2,1,0:T(8,128)(2,1)}, u32[]{:S(2)}, u32[]{:S(2)}) async-start(bf16[4,2,160,768]{3,2,1,0:T(8,128)(2,1)} %four_copies.1.refs_4_), calls=%async_computation.1 | async-start | bytes 3932160 | tf_op jit(solution)/shard_map/all_to_all | solution.py:592
  55.2 1.0 copy-start.12
  60.2 15.0 %collective-permute-start.9 = (bf16[104,2560]{1,0:T(8,128)(2,1)S(1)}, bf16[104,2560]{1,0:T(8,128)(2,1)S(1)}, u32[]{:S(2)}, u32[]{:S(2)}) collective-permute-start(bf16[104,2560]{1,0:T(8,128)(2,1)S(1)} %get-tuple-element.65), channel_id=1, source_target_pairs={{0,1},{1,2},{2,3},{3,128},{4,5},{5,6},{6,7},{7,132},{8,9},{9,10},{... | collective-permute-start | bytes 1597448 | tf_op jit(solution)/shard_map/ppermute | solution.py:47
  61.9 25.9 %collective-permute-start.10 = (bf16[104,2560]{1,0:T(8,128)(2,1)S(1)}, bf16[104,2560]{1,0:T(8,128)(2,1)S(1)}, u32[]{:S(2)}, u32[]{:S(2)}) collective-permute-start(bf16[104,2560]{1,0:T(8,128)(2,1)S(1)} %get-tuple-element.66), channel_id=1, source_target_pairs={{0,2},{1,131},{2,128},{3,1},{4,6},{5,135},{6,132},{7,5},{8,10},{9,... | collective-permute-start | bytes 1597448 | tf_op jit(solution)/shard_map/ppermute | solution.py:47
  67.5 20.4 %collective-permute-start.11 = (bf16[104,2560]{1,0:T(8,128)(2,1)S(1)}, bf16[104,2560]{1,0:T(8,128)(2,1)S(1)}, u32[]{:S(2)}, u32[]{:S(2)}) collective-permute-start(bf16[104,2560]{1,0:T(8,128)(2,1)S(1)} %get-tuple-element.67), channel_id=1, source_target_pairs={{0,131},{1,0},{2,1},{3,2},{4,135},{5,4},{6,5},{7,6},{8,139},{9,8},... | collective-permute-start | bytes 1597448 | tf_op jit(solution)/shard_map/ppermute | solution.py:47
  67.5 20.4 %collective-permute-start.3 = (bf16[104,2560]{1,0:T(8,128)(2,1)S(1)}, bf16[104,2560]{1,0:T(8,128)(2,1)S(1)}, u32[]{:S(2)}, u32[]{:S(2)}) collective-permute-start(bf16[104,2560]{1,0:T(8,128)(2,1)S(1)} %get-tuple-element.57), channel_id=1, source_target_pairs={{0,4},{1,5},{2,6},{3,7},{4,8},{5,9},{6,10},{7,11},{8,12},{9,13},{1... | collective-permute-start | bytes 1597448 | tf_op jit(solution)/shard_map/ppermute | solution.py:47
  67.5 20.4 %collective-permute-start.4 = (bf16[104,2560]{1,0:T(8,128)(2,1)S(1)}, bf16[104,2560]{1,0:T(8,128)(2,1)S(1)}, u32[]{:S(2)}, u32[]{:S(2)}) collective-permute-start(bf16[104,2560]{1,0:T(8,128)(2,1)S(1)} %get-tuple-element.58), channel_id=1, source_target_pairs={{0,8},{1,9},{2,10},{3,11},{4,12},{5,13},{6,14},{7,15},{8,0},{9,1},... | collective-permute-start | bytes 1597448 | tf_op jit(solution)/shard_map/ppermute | solution.py:47
  75.2 17.8 %collective-permute-start.5 = (bf16[104,2560]{1,0:T(8,128)(2,1)S(1)}, bf16[104,2560]{1,0:T(8,128)(2,1)S(1)}, u32[]{:S(2)}, u32[]{:S(2)}) collective-permute-start(bf16[104,2560]{1,0:T(8,128)(2,1)S(1)} %get-tuple-element.59), channel_id=1, source_target_pairs={{0,12},{1,13},{2,14},{3,15},{4,0},{5,1},{6,2},{7,3},{8,4},{9,5},{1... | collective-permute-start | bytes 1597448 | tf_op jit(solution)/shard_map/ppermute | solution.py:47
  94.3 1.4 copy-start.5
  95.7 6.4 %copy-start.6 = (bf16[416,2560]{1,0:T(8,128)(2,1)S(1)}, bf16[416,2560]{1,0:T(8,128)(2,1)}, u32[]{:S(2)}) copy-start(bf16[416,2560]{1,0:T(8,128)(2,1)} %copy-done.5) | copy-start | bytes 6389764
  95.7 6.4 %collective-permute-start.12 = (bf16[4,2,160,768]{3,2,1,0:T(8,128)(2,1)}, bf16[4,2,160,768]{3,2,1,0:T(8,128)(2,1)S(1)}, u32[]{:S(2)}, u32[]{:S(2)}) collective-permute-start(bf16[4,2,160,768]{3,2,1,0:T(8,128)(2,1)} %hold.1.refs_2_), channel_id=1, source_target_pairs={{0,16},{1,17},{2,18},{3,19},{4,20},{5,21},{6,22},{7,23},{8,24},{9,... | collective-permute-start | bytes 5898248 | tf_op jit(solution)/shard_map/ppermute | solution.py:47
  119.5 9.7 %collective-permute-start.14 = (bf16[8,160,1536]{2,1,0:T(8,128)(2,1)S(1)}, bf16[8,160,1536]{2,1,0:T(8,128)(2,1)S(1)}, u32[]{:S(2)}, u32[]{:S(2)}) collective-permute-start(bf16[8,160,1536]{2,1,0:T(8,128)(2,1)S(1)} %get-tuple-element.79), channel_id=1, source_target_pairs={{0,16},{1,17},{2,18},{3,19},{4,20},{5,21},{6,22},{7,23},{8,24},{9,... | collective-permute-start | bytes 11796488 | tf_op jit(solution)/shard_map/ppermute | solution.py:47
  128.9 4.5 %collective-permute-start.13 = (bf16[8,160,768]{2,1,0:T(8,128)(2,1)S(1)}, bf16[8,160,768]{2,1,0:T(8,128)(2,1)S(1)}, u32[]{:S(2)}, u32[]{:S(2)}) collective-permute-start(bf16[8,160,768]{2,1,0:T(8,128)(2,1)S(1)} %get-tuple-element.78), channel_id=1, source_target_pairs={{0,16},{1,17},{2,18},{3,19},{4,20},{5,21},{6,22},{7,23},{8,24},{9,... | collective-permute-start | bytes 5898248 | tf_op jit(solution)/shard_map/ppermute | solution.py:47
  129.2 6.3 %slice-start = ((s8[7864320]{0:T(1024)(128)(4,1)}), s8[4194304]{0:T(1024)(128)(4,1)S(1)}, s32[]{:S(2)}) async-start(s8[7864320]{0:T(1024)(128)(4,1)} %bitcast.17), calls=%async_computation.3 | async-start | bytes 8388608
  129.2 6.3 %slice-start.1 = ((s8[7864320]{0:T(1024)(128)(4,1)}), s8[3670016]{0:T(1024)(128)(4,1)S(1)}, s32[]{:S(2)}) async-start(s8[7864320]{0:T(1024)(128)(4,1)} %bitcast.17), calls=%async_computation.4 | async-start | bytes 7340032
  130.3 24.6 %collective-permute-start.19 = (bf16[2,160,1536]{2,1,0:T(8,128)(2,1)S(1)}, bf16[2,160,1536]{2,1,0:T(8,128)(2,1)S(1)}, u32[]{:S(2)}, u32[]{:S(2)}) collective-permute-start(bf16[2,160,1536]{2,1,0:T(8,128)(2,1)S(1)} %get-tuple-element.86), channel_id=1, source_target_pairs={{0,96},{1,97},{2,98},{3,99},{4,100},{5,101},{6,102},{7,103},{8,104... | collective-permute-start | bytes 2949128 | tf_op jit(solution)/shard_map/ppermute | solution.py:47
  133.4 24.9 %collective-permute-start.18 = (bf16[2,160,1536]{2,1,0:T(8,128)(2,1)S(1)}, bf16[2,160,1536]{2,1,0:T(8,128)(2,1)S(1)}, u32[]{:S(2)}, u32[]{:S(2)}) collective-permute-start(bf16[2,160,1536]{2,1,0:T(8,128)(2,1)S(1)} %get-tuple-element.80.refs_2_), channel_id=1, source_target_pairs={{0,32},{1,33},{2,34},{3,35},{4,36},{5,37},{6,38},{7,39},{8,40},{9,... | collective-permute-start | bytes 2949128 | tf_op jit(solution)/shard_map/ppermute | solution.py:47
  133.4 1.3 copy-start.2
  134.7 0.8 copy-start.19
  141.0 33.2 %collective-permute-start.15 = (bf16[104,2688]{1,0:T(8,128)(2,1)S(1)}, bf16[104,2688]{1,0:T(8,128)(2,1)S(1)}, u32[]{:S(2)}, u32[]{:S(2)}) collective-permute-start(bf16[104,2688]{1,0:T(8,128)(2,1)S(1)} %get-tuple-element.83), channel_id=1, source_target_pairs={{1,0},{2,1},{3,2},{128,3},{5,4},{6,5},{7,6},{132,7},{9,8},{10,9},{... | collective-permute-start | bytes 1677320 | tf_op jit(solution)/shard_map/ppermute | solution.py:47
  141.3 32.9 %collective-permute-start.16 = (bf16[104,2688]{1,0:T(8,128)(2,1)S(1)}, bf16[104,2688]{1,0:T(8,128)(2,1)S(1)}, u32[]{:S(2)}, u32[]{:S(2)}) collective-permute-start(bf16[104,2688]{1,0:T(8,128)(2,1)S(1)} %get-tuple-element.84), channel_id=1, source_target_pairs={{2,0},{131,1},{128,2},{1,3},{6,4},{135,5},{132,6},{5,7},{10,8},{13... | collective-permute-start | bytes 1677320 | tf_op jit(solution)/shard_map/ppermute | solution.py:47
  146.6 27.6 %collective-permute-start.17 = (bf16[104,2688]{1,0:T(8,128)(2,1)S(1)}, bf16[104,2688]{1,0:T(8,128)(2,1)S(1)}, u32[]{:S(2)}, u32[]{:S(2)}) collective-permute-start(bf16[104,2688]{1,0:T(8,128)(2,1)S(1)} %get-tuple-element.85), channel_id=1, source_target_pairs={{131,0},{0,1},{1,2},{2,3},{135,4},{4,5},{5,6},{6,7},{139,8},{8,9},... | collective-permute-start | bytes 1677320 | tf_op jit(solution)/shard_map/ppermute | solution.py:47
  159.2 12.4 %collective-permute-start.21 = (bf16[160,1536]{1,0:T(8,128)(2,1)S(1)}, bf16[160,1536]{1,0:T(8,128)(2,1)S(1)}, u32[]{:S(2)}, u32[]{:S(2)}) collective-permute-start(bf16[160,1536]{1,0:T(8,128)(2,1)S(1)} %get-tuple-element.88), channel_id=1, source_target_pairs={{0,96},{1,97},{2,98},{3,99},{4,100},{5,101},{6,102},{7,103},{8,104... | collective-permute-start | bytes 1474568 | tf_op jit(solution)/shard_map/ppermute | solution.py:47
  159.6 13.6 %collective-permute-start.20 = (bf16[160,1536]{1,0:T(8,128)(2,1)S(1)}, bf16[160,1536]{1,0:T(8,128)(2,1)S(1)}, u32[]{:S(2)}, u32[]{:S(2)}) collective-permute-start(bf16[160,1536]{1,0:T(8,128)(2,1)S(1)} %get-tuple-element.87.refs_6_), channel_id=1, source_target_pairs={{0,32},{1,33},{2,34},{3,35},{4,36},{5,37},{6,38},{7,39},{8,40},{9,... | collective-permute-start | bytes 1474568 | tf_op jit(solution)/shard_map/ppermute | solution.py:47
  175.6 1.4 copy-start
  177.0 0.8 copy-start.13
  177.8 45.2 %all-to-all-start.2 = ((bf16[4,104,2688]{2,1,0:T(8,128)(2,1)}), bf16[4,104,2688]{2,1,0:T(8,128)(2,1)}, u32[]{:S(2)}, u32[]{:S(2)}) async-start(bf16[4,104,2688]{2,1,0:T(8,128)(2,1)} %copy-done), calls=%async_computation.2 | async-start | bytes 4472832 | tf_op jit(solution)/shard_map/all_to_all | solution.py:610
  183.3 13.6 %collective-permute-start.23 = (bf16[2,160,768]{2,1,0:T(8,128)(2,1)}, bf16[2,160,768]{2,1,0:T(8,128)(2,1)S(1)}, u32[]{:S(2)}, u32[]{:S(2)}) collective-permute-start(bf16[2,160,768]{2,1,0:T(8,128)(2,1)} %copy-done.19), channel_id=1, source_target_pairs={{0,96},{1,97},{2,98},{3,99},{4,100},{5,101},{6,102},{7,103},{8,104... | collective-permute-start | bytes 1474568 | tf_op jit(solution)/shard_map/ppermute | solution.py:47
  183.6 13.3 %collective-permute-start.22 = (bf16[2,160,768]{2,1,0:T(8,128)(2,1)S(1)}, bf16[2,160,768]{2,1,0:T(8,128)(2,1)S(1)}, u32[]{:S(2)}, u32[]{:S(2)}) collective-permute-start(bf16[2,160,768]{2,1,0:T(8,128)(2,1)S(1)} %get-tuple-element.81.refs_4_), channel_id=1, source_target_pairs={{0,32},{1,33},{2,34},{3,35},{4,36},{5,37},{6,38},{7,39},{8,40},{9,... | collective-permute-start | bytes 1474568 | tf_op jit(solution)/shard_map/ppermute | solution.py:47
  185.3 30.9 %collective-permute-start.26 = (bf16[160,1536]{1,0:T(8,128)(2,1)}, bf16[160,1536]{1,0:T(8,128)(2,1)S(1)}, u32[]{:S(2)}, u32[]{:S(2)}) collective-permute-start(bf16[160,1536]{1,0:T(8,128)(2,1)} %copy-done.13), channel_id=1, source_target_pairs={{0,128},{1,129},{2,130},{3,131},{4,132},{5,133},{6,134},{7,135},{8... | collective-permute-start | bytes 1474568 | tf_op jit(solution)/shard_map/ppermute | solution.py:47
  196.9 1.6 copy-start.1
  198.5 1.5 copy-start.3
  200.5 17.2 %copy-start.4 = (bf16[8,160,768]{2,1,0:T(8,128)(2,1)S(1)}, bf16[8,160,768]{2,1,0:T(8,128)(2,1)}, u32[]{:S(2)}) copy-start(bf16[8,160,768]{2,1,0:T(8,128)(2,1)} %copy-done.2) | copy-start | bytes 5898244
  200.5 17.2 %collective-permute-start.25 = (bf16[160,768]{1,0:T(8,128)(2,1)S(1)}, bf16[160,768]{1,0:T(8,128)(2,1)S(1)}, u32[]{:S(2)}, u32[]{:S(2)}) collective-permute-start(bf16[160,768]{1,0:T(8,128)(2,1)S(1)} %get-tuple-element.92), channel_id=1, source_target_pairs={{0,96},{1,97},{2,98},{3,99},{4,100},{5,101},{6,102},{7,103},{8,104... | collective-permute-start | bytes 737288 | tf_op jit(solution)/shard_map/ppermute | solution.py:47
  202.1 15.6 %collective-permute-start.24 = (bf16[160,768]{1,0:T(8,128)(2,1)S(1)}, bf16[160,768]{1,0:T(8,128)(2,1)S(1)}, u32[]{:S(2)}, u32[]{:S(2)}) collective-permute-start(bf16[160,768]{1,0:T(8,128)(2,1)S(1)} %get-tuple-element.91.refs_2_), channel_id=1, source_target_pairs={{0,32},{1,33},{2,34},{3,35},{4,36},{5,37},{6,38},{7,39},{8,40},{9,... | collective-permute-start | bytes 737288 | tf_op jit(solution)/shard_map/ppermute | solution.py:47
  216.2 6.8 %copy-start.15 = (s32[128,3]{0,1:T(4,128)S(1)}, s32[128,3]{0,1:T(4,128)}, u32[]{:S(2)}) copy-start(s32[128,3]{0,1:T(4,128)} %param.8) | copy-start | bytes 4612
  217.7 1.0 copy-start.7
  218.8 4.2 %copy-start.17 = (bf16[128,3]{0,1:T(4,128)(2,1)S(1)}, bf16[128,3]{0,1:T(4,128)(2,1)}, u32[]{:S(2)}) copy-start(bf16[128,3]{0,1:T(4,128)(2,1)} %param.9) | copy-start | bytes 2308
  219.4 12.1 %collective-permute-start.27 = (bf16[160,768]{1,0:T(8,128)(2,1)S(1)}, bf16[160,768]{1,0:T(8,128)(2,1)S(1)}, u32[]{:S(2)}, u32[]{:S(2)}) collective-permute-start(bf16[160,768]{1,0:T(8,128)(2,1)S(1)} %get-tuple-element.94.refs_5_), channel_id=1, source_target_pairs={{0,128},{1,129},{2,130},{3,131},{4,132},{5,133},{6,134},{7,135},{8... | collective-permute-start | bytes 737288 | tf_op jit(solution)/shard_map/ppermute | solution.py:47
  231.5 1.1 copy-start.8
where the time goes:
time: 234 us; the launch traced here: 233 us
  waiting for transfers between devices  80.3 us (34%)
  starting transfers between devices  74 us (32%)
  Pallas kernels  59.5 us (25%)
  local copies, waits for them, and re-layouts  16.7 us (7%)
    ppermute x28, waiting for transfers between devices, send(): return lax.ppermute(v, AXES, pairs)  67.4 us
    ppermute x28, starting transfers between devices, send(): return lax.ppermute(v, AXES, pairs)  56.5 us
    pallas_call x19, Pallas kernels, call(): pl.pallas_call(body, out_shape=out_shape, in_specs=specs, out_specs=out_s...  46.7 us
    unnamed x44, local copies, waits for them, and re-layouts  16.6 us
    all_to_all x1, waiting for transfers between devices, on_device(): wd_zh = lax.all_to_all(wd_two, 'zh', 0, 0, tiled=True)  12.9 us
    all_to_all x1, starting transfers between devices, on_device(): wd_zh = lax.all_to_all(wd_two, 'zh', 0, 0, tiled=True)  7.56 us
    pallas_call x1, Pallas kernels, down_part(): pl.pallas_call(functools.partial(down_kernel, part), out_shape=[jax.Shape...  6.46 us
    pallas_call x1, Pallas kernels, up_part(): pl.pallas_call(up_kernel, grid=(steps,), out_shape=[jax.ShapeDtypeStruct(...  6.42 us
  transfers between devices with their start and end apart: 31, of which 13 were waited for; matrix products, arithmetic and copies ran while one was open for 0% of the time, Pallas kernels for 16%

commit v1 on v0

--- a/solution.py
+++ b/solution.py
@@ -158,21 +158,22 @@
     )
 
 
-def copies_kernel(v, out):
+def pair_kernel(own, far, out):
     for k in range(4):
-        out[k] = v[...]
-
-
-def four_copies(v, deps):
-    return call(
-        copies_kernel,
-        (v,),
-        [VMEM],
-        jax.ShapeDtypeStruct((4,) + v.shape, BF),
+        out[k, 0] = own[...]
+        out[k, 1] = far[...]
+
+
+def pair_parts(own, far, deps):
+    return call(
+        pair_kernel,
+        (own, far),
+        [VMEM] * 2,
+        jax.ShapeDtypeStruct((4, 2) + own.shape, BF),
         VMEM,
         deps,
-        cost_estimate=cost(0, 10 * v.size),
-        name="four_copies",
+        cost_estimate=cost(0, 20 * own.size),
+        name="pair_parts",
     )
 
 
@@ -222,16 +223,17 @@
     )
 
 
-def hold(v, deps):
+def hold(arrays, deps):
     anys = pl.BlockSpec(memory_space=pl.ANY)
-    return call(
-        lambda v_ref, out_ref: None,
-        (v,),
-        [anys],
-        jax.ShapeDtypeStruct(v.shape, v.dtype),
-        anys,
-        deps,
-        input_output_aliases={0: 0},
+    count = len(arrays)
+    return call(
+        lambda *refs: None,
+        arrays,
+        [anys] * count,
+        [jax.ShapeDtypeStruct(v.shape, v.dtype) for v in arrays],
+        [anys] * count,
+        deps,
+        input_output_aliases={k: k for k in range(count)},
         name="hold",
     )
 
@@ -312,7 +314,7 @@
     hid = hidden.shape[1]
     part = w_own.shape[2]
     w_spec = pl.BlockSpec(
-        (2, 1, part, hid), lambda b, p: (lax.rem(b, 2), lax.div(b, 2), 0, 0)
+        (2, 1, part, hid), lambda b, p: (lax.rem(b, 2), lax.rem(lax.div(b, 2) + p[2], 2), 0, 0)
     )
     anys = pl.BlockSpec(memory_space=pl.ANY)
     whole = lambda *shape: pl.BlockSpec(shape, lambda b, p: (0,) * len(shape))
@@ -577,22 +579,25 @@
     ids_t, w_t = expert_ids.T, route_weights.T
 
     wd = w_down[0].T
-    wd_two = jnp.stack([wd, wd])
-    wd_zh = lax.all_to_all(wd_two, "zh", 0, 0, tiled=True)
-    made = prep(pos, ids_t, w_t, layer_inputs, cotangent, [wd_two])
+    wd_far = send(wd, shift(dz=4))
+    made = prep(pos, ids_t, w_t, layer_inputs, cotangent, [])
     rows, ogs, sel = made[:4], made[4:8], made[8]
     z_moves = [z_window(d) for d in (1, 2, 3)]
     x_moves = [shift(dx=d) for d in (1, 2, 3)]
-    over = lambda blocks, moves: [blocks[0]] + [send(b, m) for b, m in zip(blocks[1:], moves)]
+
+    def over(blocks, moves):
+        got = {d: send(blocks[d], moves[d - 1]) for d in (1, 3, 2)}
+        return [blocks[0]] + [got[d] for d in (1, 2, 3)]
+
     home = lambda blocks, moves: over(blocks, [back(m) for m in moves])
     flip = lambda v: send(v, shift(dc=1))
-    rows = over(rows, z_moves)
-    pairs = four_copies(wd_zh, [rows[1]])
+    rows = over([rows[0], *hold(list(rows[1:]), [wd_far])], z_moves)
+    pairs = pair_parts(wd, wd_far, [rows[1]])
     rows = regroup(rows, 512, [pairs])
     wd_own = lax.all_to_all(pairs, "y", 0, 0, tiled=True)
     ogs = regroup(over(ogs, x_moves), 512, [rows[0]])
     xs, og = assemble(over(rows, x_moves), over(ogs, z_moves), [])
-    wd_own = hold(wd_own, [xs])
+    (wd_own,) = hold([wd_own], [xs])
     wd_other = flip(wd_own)
 
     hidden, ca, cb = up_part(xs, w_gate_up)

time: 234 us -> 224 us (0.957)
  the two profiles are of different devices: /device:TPU:6 before, /device:TPU:34 now
where the time goes in v1:
time: 224 us; the launch traced here: 223 us
  waiting for transfers between devices  91.9 us (41%)
  Pallas kernels  62.1 us (28%)
  starting transfers between devices  48.1 us (21%)
  local copies, waits for them, and re-layouts  20.3 us (9%)
    ppermute x29, waiting for transfers between devices, send(): return lax.ppermute(v, AXES, pairs)  91.8 us
    pallas_call x20, Pallas kernels, call(): pl.pallas_call(body, out_shape=out_shape, in_specs=specs, out_specs=out_s...  49.3 us
    ppermute x29, starting transfers between devices, send(): return lax.ppermute(v, AXES, pairs)  39.2 us
    unnamed x54, local copies, waits for them, and re-layouts  20.2 us
    pallas_call x1, Pallas kernels, down_part(): pl.pallas_call(functools.partial(down_kernel, part), out_shape=[jax.Shape...  6.61 us
    pallas_call x1, Pallas kernels, up_part(): pl.pallas_call(up_kernel, grid=(steps,), out_shape=[jax.ShapeDtypeStruct(...  6.25 us
  transfers between devices with their start and end apart: 31, of which 15 were waited for; matrix products, arithmetic and copies ran while one was open for 0% of the time, Pallas kernels for 19%

profile of v1, /device:TPU:34, one launch (start us, length us, event | category | flops | bytes accessed | tf_op | source)
XLA Modules:
  0.0 223.3 jit_solution(12073373840913361230)
XLA Ops:
  0.6 6.4 %collective-permute-start = (bf16[160,768]{1,0:T(8,128)(2,1)}, bf16[160,768]{1,0:T(8,128)(2,1)S(1)}, u32[]{:S(2)}, u32[]{:S(2)}) collective-permute-start(bf16[160,768]{1,0:T(8,128)(2,1)} %bitcast.18), channel_id=1, source_target_pairs={{0,128},{1,129},{2,130},{3,131},{4,132},{5,133},{6,134},{7,135},{8... | collective-permute-start | bytes 737288 | tf_op jit(solution)/shard_map/ppermute | solution.py:47
  7.1 1.1 copy-done.12
  8.2 1.1 copy-done.13
  10.7 2.9 %prep.1 = (bf16[104,2560]{1,0:T(8,128)(2,1)S(1)}, bf16[104,2560]{1,0:T(8,128)(2,1)S(1)}, bf16[104,2560]{1,0:T(8,128)(2,1)S(1)}, bf16[104,2560]{1,0:T(8,128)(2,1)...) custom-call(s32[13]{0:T(128)S(1)} %concatenate.3.refs_0_, ...), custom_call_target="tpu_custom_call" | custom-call | flops 8519680 | bytes 87040 | tf_op jit(solution)/shard_map/prep/pallas_call | solution.py:108
  13.6 0.8 copy-done.16
  14.4 4.2 %collective-permute-done.refs_3_.refs_1_ = bf16[160,768]{1,0:T(8,128)(2,1)S(1)} collective-permute-done((bf16[160,768]{1,0:T(8,128)(2,1)}, bf16[160,768]{1,0:T(8,128)(2,1)S(1)}, u32[]{:S(2)}, u32[]{:S(2)}) %collective-permute-start) | collective-permute-done | bytes 245792 | tf_op jit(solution)/shard_map/ppermute | solution.py:47
  18.5 1.4 collective-permute-start.1
  19.9 1.5 collective-permute-start.7
  21.4 1.1 collective-permute-start.2
  22.9 1.1 collective-permute-start.8
  24.0 9.6 %collective-permute-done.1.refs_2_.refs_1_ = bf16[104,2560]{1,0:T(8,128)(2,1)S(1)} collective-permute-done((bf16[104,2560]{1,0:T(8,128)(2,1)S(1)}, bf16[104,2560]{1,0:T(8,128)(2,1)S(1)}, u32[]{:S(2)}, u32[]{:S(2)}) %collective-permute-start.1) | collective-permute-done | bytes 532512 | tf_op jit(solution)/shard_map/ppermute | solution.py:47
  34.1 1.5 pair_parts.1.refs_4_
  35.6 4.5 %all-to-all-start = ((bf16[4,2,160,768]{3,2,1,0:T(8,128)(2,1)}), bf16[4,2,160,768]{3,2,1,0:T(8,128)(2,1)}, u32[]{:S(2)}, u32[]{:S(2)}) async-start(bf16[4,2,160,768]{3,2,1,0:T(8,128)(2,1)} %pair_parts.1.refs_4_), calls=%async_computation | async-start | bytes 3932160 | tf_op jit(solution)/shard_map/all_to_all | solution.py:597
  40.1 6.4 %collective-permute-done.3.refs_3_ = bf16[104,2560]{1,0:T(8,128)(2,1)} collective-permute-done((bf16[104,2560]{1,0:T(8,128)(2,1)}, bf16[104,2560]{1,0:T(8,128)(2,1)}, u32[]{:S(2)}, u32[]{:S(2)}) %collective-permute-start.3) | collective-permute-done | bytes 532512 | tf_op jit(solution)/shard_map/ppermute | solution.py:47
  46.4 1.0 copy-done.17
  47.5 3.3 %regroup.3 = (bf16[104,2560]{1,0:T(8,128)(2,1)S(1)}, bf16[104,2560]{1,0:T(8,128)(2,1)S(1)}, bf16[104,2560]{1,0:T(8,128)(2,1)S(1)}, bf16[104,2560]{1,0:T(8,128)(2,1)S(1)}) custom-call(bf16[104,2560]{1,0:T(8,128)(2,1)S(1)} %copy-done.17, bf16[104,2560]{1,0:T(8,128)(2,1)S(1)} %collective-permute-done.1.refs_2_.refs_1_, ...), custom_call_target="tpu_custom_call" | custom-call | bytes 66560 | tf_op jit(solution)/shard_map/regroup/pallas_call | solution.py:108
  50.8 3.4 %regroup.4 = (bf16[104,2560]{1,0:T(8,128)(2,1)S(1)}, bf16[104,2560]{1,0:T(8,128)(2,1)S(1)}, bf16[104,2560]{1,0:T(8,128)(2,1)S(1)}, bf16[104,2560]{1,0:T(8,128)(2,1)S(1)}) custom-call(bf16[104,2560]{1,0:T(8,128)(2,1)S(1)} %copy-done.15, bf16[104,2560]{1,0:T(8,128)(2,1)} %collective-permute-done.7.refs_1_, bf16[104,2560]{1,0:T(8,128)(2,1)} %collective-permute-done.8.refs_2_, ...), custom_call_target="tpu_custom_call" | custom-call | bytes 66560 | tf_op jit(solution)/shard_map/regroup/pallas_call | solution.py:108
  54.2 1.1 collective-permute-start.10
  55.3 3.5 %collective-permute-start.11 = (bf16[104,2560]{1,0:T(8,128)(2,1)S(1)}, bf16[104,2560]{1,0:T(8,128)(2,1)S(1)}, u32[]{:S(2)}, u32[]{:S(2)}) collective-permute-start(bf16[104,2560]{1,0:T(8,128)(2,1)S(1)} %get-tuple-element.72), channel_id=1, source_target_pairs={{0,2},{1,131},{2,128},{3,1},{4,6},{5,135},{6,132},{7,5},{8,10},{9,... | collective-permute-start | bytes 1597448 | tf_op jit(solution)/shard_map/ppermute | solution.py:47
  59.3 1.2 collective-permute-start.4
  60.5 1.4 collective-permute-start.5
  61.9 7.3 %collective-permute-done.10.refs_5_ = bf16[104,2560]{1,0:T(8,128)(2,1)S(1)} collective-permute-done((bf16[104,2560]{1,0:T(8,128)(2,1)S(1)}, bf16[104,2560]{1,0:T(8,128)(2,1)S(1)}, u32[]{:S(2)}, u32[]{:S(2)}) %collective-permute-start.10) | collective-permute-done | bytes 532512 | tf_op jit(solution)/shard_map/ppermute | solution.py:47
  69.8 1.6 collective-permute-done.11.refs_6_
  71.3 10.2 %collective-permute-done.12.refs_7_ = bf16[104,2560]{1,0:T(8,128)(2,1)S(1)} collective-permute-done((bf16[104,2560]{1,0:T(8,128)(2,1)S(1)}, bf16[104,2560]{1,0:T(8,128)(2,1)S(1)}, u32[]{:S(2)}, u32[]{:S(2)}) %collective-permute-start.12) | collective-permute-done | bytes 532512 | tf_op jit(solution)/shard_map/ppermute | solution.py:47
  81.5 4.8 %collective-permute-done.6.refs_3_ = bf16[104,2560]{1,0:T(8,128)(2,1)S(1)} collective-permute-done((bf16[104,2560]{1,0:T(8,128)(2,1)S(1)}, bf16[104,2560]{1,0:T(8,128)(2,1)S(1)}, u32[]{:S(2)}, u32[]{:S(2)}) %collective-permute-start.6) | collective-permute-done | bytes 532512 | tf_op jit(solution)/shard_map/ppermute | solution.py:47
  86.3 1.2 assemble.1
  87.5 1.4 copy-done.2
  88.9 1.3 copy-done.8
  90.3 1.6 copy-done.3
  91.9 1.6 copy-done.4
  93.5 6.3 %up_part.1 = (bf16[416,768]{1,0:T(8,128)(2,1)S(1)}, f32[416,768]{1,0:T(8,128)S(1)}, f32[416,768]{1,0:T(8,128)S(1)}) custom-call(bf16[416,2560]{1,0:T(8,128)(2,1)S(1)} %copy-done.4, bf16[1,2560,1536]{2,1,0:T(8,128)(2,1)} %refs_2_.1, bf16[1,2560,1536]{2,1,0:T(8,128)(2,1)} %refs_2_.1), custom_call_target="tpu_custom_call" | custom-call | flops 51118080 | bytes 156160 | tf_op jit(solution)/shard_map/up_part/pallas_call | solution.py:258
  99.7 6.6 %down_part.1 = (bf16[416,768]{1,0:T(8,128)(2,1)S(1)}, bf16[416,768]{1,0:T(8,128)(2,1)S(1)}, f32[416,128]{1,0:T(8,128)S(1)}) custom-call(s32[13]{0:T(128)S(1)} %concatenate.3.refs_0_, bf16[416,2560]{1,0:T(8,128)(2,1)S(1)} %copy-done.9, bf16[4,2,160,768]{3,2,1,0:T(8,128)(2,1)} %hold.3.refs_2_, bf16[4,2,160,768]{3,2,1,0:T(8,128)(2,1)S(1)} %collective-permute-done.13.refs_3_, ...), custom_call_target="tpu_custom_call" | custom-call | flops 25559040 | bytes 94720 | tf_op jit(solution)/shard_map/down_part/pallas_call | solution.py:321
  106.4 10.9 %grad_part.2 = (bf16[8,160,1536]{2,1,0:T(8,128)(2,1)S(1)}, bf16[8,160,1536]{2,1,0:T(8,128)(2,1)S(1)}) custom-call(s32[13]{0:T(128)S(1)} %concatenate.3.refs_0_, bf16[416,2560]{1,0:T(8,128)(2,1)S(1)} %copy-done.4, bf16[416,768]{1,0:T(8,128)(2,1)S(1)} %get-tuple-element.79.refs_2_.refs_0_, bf16[416,768]{1,0:T(8,128)(2,1)S(1)} %get-tuple-element.80.refs_3_.refs_1_), custom_call_target="tpu_custom_call" | custom-call | flops 51118080 | bytes 156160 | tf_op jit(solution)/shard_map/grad_part/pallas_call | solution.py:108
  117.3 9.0 %grad_part.3 = (bf16[8,160,768]{2,1,0:T(8,128)(2,1)S(1)}, bf16[8,160,768]{2,1,0:T(8,128)(2,1)S(1)}) custom-call(s32[13]{0:T(128)S(1)} %concatenate.3.refs_0_, bf16[416,2560]{1,0:T(8,128)(2,1)S(1)} %copy-done.9, bf16[416,768]{1,0:T(8,128)(2,1)S(1)} %get-tuple-element.76.refs_4_.refs_2_, bf16[8,160,1536]{2,1,0:T(8,128)(2,1)S(1)} %get-tuple-element.82.refs_3_.refs_0_), custom_call_target="tpu_custom_call" | custom-call | flops 25559040 | bytes 94720 | tf_op jit(solution)/shard_map/grad_part/pallas_call | solution.py:108
  126.9 1.1 first_sum.2
  128.1 3.1 %collective-permute-start.20 = (bf16[2,160,1536]{2,1,0:T(8,128)(2,1)S(1)}, bf16[2,160,1536]{2,1,0:T(8,128)(2,1)S(1)}, u32[]{:S(2)}, u32[]{:S(2)}) collective-permute-start(bf16[2,160,1536]{2,1,0:T(8,128)(2,1)S(1)} %get-tuple-element.92), channel_id=1, source_target_pairs={{0,96},{1,97},{2,98},{3,99},{4,100},{5,101},{6,102},{7,103},{8,104... | collective-permute-start | bytes 2949128 | tf_op jit(solution)/shard_map/ppermute | solution.py:47
  133.3 5.5 %row_part.1 = (bf16[104,2688]{1,0:T(8,128)(2,1)S(1)}, bf16[104,2688]{1,0:T(8,128)(2,1)S(1)}, bf16[104,2688]{1,0:T(8,128)(2,1)S(1)}, bf16[104,2688]{1,0:T(8,128)(2,1)S(1)}) custom-call(bf16[416,768]{1,0:T(8,128)(2,1)S(1)} %get-tuple-element.79.refs_2_.refs_0_, bf16[416,768]{1,0:T(8,128)(2,1)S(1)} %get-tuple-element.80.refs_3_.refs_1_, ...), custom_call_target="tpu_custom_call" | custom-call | flops 51118080 | bytes 152832 | tf_op jit(solution)/shard_map/row_part/pallas_call | solution.py:108
  139.5 1.4 collective-permute-start.17
  140.9 1.1 collective-permute-start.18
  142.0 10.4 %collective-permute-done.20.refs_3_ = bf16[2,160,1536]{2,1,0:T(8,128)(2,1)S(1)} collective-permute-done((bf16[2,160,1536]{2,1,0:T(8,128)(2,1)S(1)}, bf16[2,160,1536]{2,1,0:T(8,128)(2,1)S(1)}, u32[]{:S(2)}, u32[]{:S(2)}) %collective-permute-start.20) | collective-permute-done | bytes 983072 | tf_op jit(solution)/shard_map/ppermute | solution.py:47
  152.4 3.4 %collective-permute-done.19.refs_2_ = bf16[2,160,1536]{2,1,0:T(8,128)(2,1)S(1)} collective-permute-done((bf16[2,160,1536]{2,1,0:T(8,128)(2,1)S(1)}, bf16[2,160,1536]{2,1,0:T(8,128)(2,1)S(1)}, u32[]{:S(2)}, u32[]{:S(2)}) %collective-permute-start.19) | collective-permute-done | bytes 983072 | tf_op jit(solution)/shard_map/ppermute | solution.py:47
  155.8 0.9 second_sum.2
  157.0 1.7 collective-permute-start.21
  158.8 10.0 %collective-permute-done.22.refs_5_ = bf16[160,1536]{1,0:T(8,128)(2,1)S(1)} collective-permute-done((bf16[160,1536]{1,0:T(8,128)(2,1)S(1)}, bf16[160,1536]{1,0:T(8,128)(2,1)S(1)}, u32[]{:S(2)}, u32[]{:S(2)}) %collective-permute-start.22) | collective-permute-done | bytes 491552 | tf_op jit(solution)/shard_map/ppermute | solution.py:47
  168.8 1.5 collective-permute-done.21.refs_4_
  170.3 1.1 far_sum.2
  171.4 1.3 regroup.5.refs_4_
  172.8 1.4 copy-done
  175.0 4.5 %all-to-all-start.1 = ((bf16[4,104,2688]{2,1,0:T(8,128)(2,1)}), bf16[4,104,2688]{2,1,0:T(8,128)(2,1)}, u32[]{:S(2)}, u32[]{:S(2)}) async-start(bf16[4,104,2688]{2,1,0:T(8,128)(2,1)} %copy-done), calls=%async_computation.1 | async-start | bytes 4472832 | tf_op jit(solution)/shard_map/all_to_all | solution.py:615
  179.8 1.7 collective-permute-start.23
  181.6 2.6 %collective-permute-start.27 = (bf16[160,1536]{1,0:T(8,128)(2,1)}, bf16[160,1536]{1,0:T(8,128)(2,1)S(1)}, u32[]{:S(2)}, u32[]{:S(2)}) collective-permute-start(bf16[160,1536]{1,0:T(8,128)(2,1)} %copy-done.18), channel_id=1, source_target_pairs={{0,128},{1,129},{2,130},{3,131},{4,132},{5,133},{6,134},{7,135},{8... | collective-permute-start | bytes 1474568 | tf_op jit(solution)/shard_map/ppermute | solution.py:47
  184.1 6.7 %collective-permute-done.24.refs_3_ = bf16[2,160,768]{2,1,0:T(8,128)(2,1)S(1)} collective-permute-done((bf16[2,160,768]{2,1,0:T(8,128)(2,1)}, bf16[2,160,768]{2,1,0:T(8,128)(2,1)S(1)}, u32[]{:S(2)}, u32[]{:S(2)}) %collective-permute-start.24) | collective-permute-done | bytes 491552 | tf_op jit(solution)/shard_map/ppermute | solution.py:47
  190.9 1.3 collective-permute-done.23.refs_2_
  192.2 1.6 copy-done.1
  193.8 1.5 copy-done.6
  196.4 1.5 collective-permute-start.25
  197.9 8.9 %collective-permute-done.27.refs_1_ = bf16[160,1536]{1,0:T(8,128)(2,1)S(1)} collective-permute-done((bf16[160,1536]{1,0:T(8,128)(2,1)}, bf16[160,1536]{1,0:T(8,128)(2,1)S(1)}, u32[]{:S(2)}, u32[]{:S(2)}) %collective-permute-start.27) | collective-permute-done | bytes 491552 | tf_op jit(solution)/shard_map/ppermute | solution.py:47
  206.8 1.5 last_sum.2.refs_6_
  208.3 1.0 copy-done.10
  209.9 2.7 %collective-permute-start.28 = (bf16[160,768]{1,0:T(8,128)(2,1)S(1)}, bf16[160,768]{1,0:T(8,128)(2,1)S(1)}, u32[]{:S(2)}, u32[]{:S(2)}) collective-permute-start(bf16[160,768]{1,0:T(8,128)(2,1)S(1)} %get-tuple-element.100.refs_5_), channel_id=1, source_target_pairs={{0,128},{1,129},{2,130},{3,131},{4,132},{5,133},{6,134},{7,135},{8... | collective-permute-start | bytes 737288 | tf_op jit(solution)/shard_map/ppermute | solution.py:47
  212.6 3.3 %final.1 = (bf16[128,2560]{1,0:T(8,128)(2,1)}, bf16[3,128]{1,0:T(4,128)(2,1)}) custom-call(s32[13]{0:T(128)S(1)} %concatenate.3.refs_0_, s32[3,128]{1,0:T(4,128)S(1)} %bitcast.21, bf16[3,128]{1,0:T(4,128)(2,1)S(1)} %bitcast.23, bf16[416,128]{1,0:T(8,128)(2,1)S(1)} %get-tuple-element.54.refs_3_, bf16[4,104,2688]{2,1,0:T(8,128)(2,1)} %all-to-all-done.1.refs_4_, ...), custom_call_target="tpu_custom_call" | custom-call | flops 4259840 | bytes 43520 | tf_op jit(solution)/shard_map/final/pallas_call | solution.py:108
  215.9 5.6 %collective-permute-done.28.refs_1_ = bf16[160,768]{1,0:T(8,128)(2,1)S(1)} collective-permute-done((bf16[160,768]{1,0:T(8,128)(2,1)S(1)}, bf16[160,768]{1,0:T(8,128)(2,1)S(1)}, u32[]{:S(2)}, u32[]{:S(2)}) %collective-permute-start.28) | collective-permute-done | bytes 245792 | tf_op jit(solution)/shard_map/ppermute | solution.py:47
  221.5 1.1 copy-done.11
  222.5 0.8 last_sum.3
  (77 shorter events, 10.1 us)
Async XLA Ops:
  0.6 17.9 %collective-permute-start = (bf16[160,768]{1,0:T(8,128)(2,1)}, bf16[160,768]{1,0:T(8,128)(2,1)S(1)}, u32[]{:S(2)}, u32[]{:S(2)}) collective-permute-start(bf16[160,768]{1,0:T(8,128)(2,1)} %bitcast.18), channel_id=1, source_target_pairs={{0,128},{1,129},{2,130},{3,131},{4,132},{5,133},{6,134},{7,135},{8... | collective-permute-start | bytes 737288 | tf_op jit(solution)/shard_map/ppermute | solution.py:47
  7.1 1.1 copy-start.12
  8.2 1.1 copy-start.13
  9.3 0.7 copy-start.20
  10.0 0.7 copy-start.22
  10.7 23.5 %copy-start.19 = (bf16[1,768,160]{1,2,0:T(8,128)(2,1)S(1)}, bf16[1,768,160]{1,2,0:T(8,128)(2,1)}, u32[]{:S(2)}) copy-start(bf16[1,768,160]{1,2,0:T(8,128)(2,1)} %param.11) | copy-start | bytes 737284
  13.6 0.8 copy-start.16
  14.4 19.2 %copy-start.14 = (bf16[104,2560]{1,0:T(8,128)(2,1)}, bf16[104,2560]{1,0:T(8,128)(2,1)S(1)}, u32[]{:S(2)}) copy-start(bf16[104,2560]{1,0:T(8,128)(2,1)S(1)} %get-tuple-element.66.refs_0_) | copy-start | bytes 1597444
  18.5 15.0 %collective-permute-start.1 = (bf16[104,2560]{1,0:T(8,128)(2,1)S(1)}, bf16[104,2560]{1,0:T(8,128)(2,1)S(1)}, u32[]{:S(2)}, u32[]{:S(2)}) collective-permute-start(bf16[104,2560]{1,0:T(8,128)(2,1)S(1)} %get-tuple-element.59), channel_id=1, source_target_pairs={{0,1},{1,2},{2,3},{3,128},{4,5},{5,6},{6,7},{7,132},{8,9},{9,10},{... | collective-permute-start | bytes 1597448 | tf_op jit(solution)/shard_map/ppermute | solution.py:47
  19.9 30.9 %collective-permute-start.7 = (bf16[104,2560]{1,0:T(8,128)(2,1)}, bf16[104,2560]{1,0:T(8,128)(2,1)}, u32[]{:S(2)}, u32[]{:S(2)}) collective-permute-start(bf16[104,2560]{1,0:T(8,128)(2,1)} %get-tuple-element.67), channel_id=1, source_target_pairs={{0,4},{1,5},{2,6},{3,7},{4,8},{5,9},{6,10},{7,11},{8,12},{9,13},{1... | collective-permute-start | bytes 1597448 | tf_op jit(solution)/shard_map/ppermute | solution.py:47
  21.4 18.7 %collective-permute-start.2 = (bf16[104,2560]{1,0:T(8,128)(2,1)S(1)}, bf16[104,2560]{1,0:T(8,128)(2,1)}, u32[]{:S(2)}, u32[]{:S(2)}) collective-permute-start(bf16[104,2560]{1,0:T(8,128)(2,1)S(1)} %get-tuple-element.60), channel_id=1, source_target_pairs={{0,2},{1,131},{2,128},{3,1},{4,6},{5,135},{6,132},{7,5},{8,10},{9,... | collective-permute-start | bytes 1597448 | tf_op jit(solution)/shard_map/ppermute | solution.py:47
  22.5 24.0 %collective-permute-start.3 = (bf16[104,2560]{1,0:T(8,128)(2,1)}, bf16[104,2560]{1,0:T(8,128)(2,1)}, u32[]{:S(2)}, u32[]{:S(2)}) collective-permute-start(bf16[104,2560]{1,0:T(8,128)(2,1)} %get-tuple-element.61), channel_id=1, source_target_pairs={{0,131},{1,0},{2,1},{3,2},{4,135},{5,4},{6,5},{7,6},{8,139},{9,8},... | collective-permute-start | bytes 1597448 | tf_op jit(solution)/shard_map/ppermute | solution.py:47
  22.9 27.9 %collective-permute-start.8 = (bf16[104,2560]{1,0:T(8,128)(2,1)S(1)}, bf16[104,2560]{1,0:T(8,128)(2,1)}, u32[]{:S(2)}, u32[]{:S(2)}) collective-permute-start(bf16[104,2560]{1,0:T(8,128)(2,1)S(1)} %get-tuple-element.68), channel_id=1, source_target_pairs={{0,8},{1,9},{2,10},{3,11},{4,12},{5,13},{6,14},{7,15},{8,0},{9,1},... | collective-permute-start | bytes 1597448 | tf_op jit(solution)/shard_map/ppermute | solution.py:47
  33.6 17.2 %collective-permute-start.9 = (bf16[104,2560]{1,0:T(8,128)(2,1)S(1)}, bf16[104,2560]{1,0:T(8,128)(2,1)}, u32[]{:S(2)}, u32[]{:S(2)}) collective-permute-start(bf16[104,2560]{1,0:T(8,128)(2,1)S(1)} %get-tuple-element.69), channel_id=1, source_target_pairs={{0,12},{1,13},{2,14},{3,15},{4,0},{5,1},{6,2},{7,3},{8,4},{9,5},{1... | collective-permute-start | bytes 1597448 | tf_op jit(solution)/shard_map/ppermute | solution.py:47
  35.6 54.7 %all-to-all-start = ((bf16[4,2,160,768]{3,2,1,0:T(8,128)(2,1)}), bf16[4,2,160,768]{3,2,1,0:T(8,128)(2,1)}, u32[]{:S(2)}, u32[]{:S(2)}) async-start(bf16[4,2,160,768]{3,2,1,0:T(8,128)(2,1)} %pair_parts.1.refs_4_), calls=%async_computation | async-start | bytes 3932160 | tf_op jit(solution)/shard_map/all_to_all | solution.py:597
  46.4 1.0 copy-start.17
  47.5 3.3 %copy-start.15 = (bf16[104,2560]{1,0:T(8,128)(2,1)S(1)}, bf16[104,2560]{1,0:T(8,128)(2,1)}, u32[]{:S(2)}) copy-start(bf16[104,2560]{1,0:T(8,128)(2,1)} %copy-done.14) | copy-start | bytes 1597444
  54.2 15.0 %collective-permute-start.10 = (bf16[104,2560]{1,0:T(8,128)(2,1)S(1)}, bf16[104,2560]{1,0:T(8,128)(2,1)S(1)}, u32[]{:S(2)}, u32[]{:S(2)}) collective-permute-start(bf16[104,2560]{1,0:T(8,128)(2,1)S(1)} %get-tuple-element.71), channel_id=1, source_target_pairs={{0,1},{1,2},{2,3},{3,128},{4,5},{5,6},{6,7},{7,132},{8,9},{9,10},{... | collective-permute-start | bytes 1597448 | tf_op jit(solution)/shard_map/ppermute | solution.py:47
  55.3 16.0 %collective-permute-start.11 = (bf16[104,2560]{1,0:T(8,128)(2,1)S(1)}, bf16[104,2560]{1,0:T(8,128)(2,1)S(1)}, u32[]{:S(2)}, u32[]{:S(2)}) collective-permute-start(bf16[104,2560]{1,0:T(8,128)(2,1)S(1)} %get-tuple-element.72), channel_id=1, source_target_pairs={{0,2},{1,131},{2,128},{3,1},{4,6},{5,135},{6,132},{7,5},{8,10},{9,... | collective-permute-start | bytes 1597448 | tf_op jit(solution)/shard_map/ppermute | solution.py:47
  58.8 22.7 %collective-permute-start.12 = (bf16[104,2560]{1,0:T(8,128)(2,1)S(1)}, bf16[104,2560]{1,0:T(8,128)(2,1)S(1)}, u32[]{:S(2)}, u32[]{:S(2)}) collective-permute-start(bf16[104,2560]{1,0:T(8,128)(2,1)S(1)} %get-tuple-element.73), channel_id=1, source_target_pairs={{0,131},{1,0},{2,1},{3,2},{4,135},{5,4},{6,5},{7,6},{8,139},{9,8},... | collective-permute-start | bytes 1597448 | tf_op jit(solution)/shard_map/ppermute | solution.py:47
  59.3 22.2 %collective-permute-start.4 = (bf16[104,2560]{1,0:T(8,128)(2,1)S(1)}, bf16[104,2560]{1,0:T(8,128)(2,1)S(1)}, u32[]{:S(2)}, u32[]{:S(2)}) collective-permute-start(bf16[104,2560]{1,0:T(8,128)(2,1)S(1)} %get-tuple-element.63), channel_id=1, source_target_pairs={{0,4},{1,5},{2,6},{3,7},{4,8},{5,9},{6,10},{7,11},{8,12},{9,13},{1... | collective-permute-start | bytes 1597448 | tf_op jit(solution)/shard_map/ppermute | solution.py:47
  60.5 21.0 %collective-permute-start.5 = (bf16[104,2560]{1,0:T(8,128)(2,1)S(1)}, bf16[104,2560]{1,0:T(8,128)(2,1)S(1)}, u32[]{:S(2)}, u32[]{:S(2)}) collective-permute-start(bf16[104,2560]{1,0:T(8,128)(2,1)S(1)} %get-tuple-element.64), channel_id=1, source_target_pairs={{0,8},{1,9},{2,10},{3,11},{4,12},{5,13},{6,14},{7,15},{8,0},{9,1},... | collective-permute-start | bytes 1597448 | tf_op jit(solution)/shard_map/ppermute | solution.py:47
  69.2 17.1 %collective-permute-start.6 = (bf16[104,2560]{1,0:T(8,128)(2,1)S(1)}, bf16[104,2560]{1,0:T(8,128)(2,1)S(1)}, u32[]{:S(2)}, u32[]{:S(2)}) collective-permute-start(bf16[104,2560]{1,0:T(8,128)(2,1)S(1)} %get-tuple-element.65), channel_id=1, source_target_pairs={{0,12},{1,13},{2,14},{3,15},{4,0},{5,1},{6,2},{7,3},{8,4},{9,5},{1... | collective-permute-start | bytes 1597448 | tf_op jit(solution)/shard_map/ppermute | solution.py:47
  87.5 1.4 copy-start.2
  88.9 1.3 copy-start.8
  90.2 1.6 copy-start.3
  91.9 1.6 copy-start.4
  91.9 7.9 %copy-start.9 = (bf16[416,2560]{1,0:T(8,128)(2,1)S(1)}, bf16[416,2560]{1,0:T(8,128)(2,1)}, u32[]{:S(2)}) copy-start(bf16[416,2560]{1,0:T(8,128)(2,1)} %copy-done.8) | copy-start | bytes 6389764
  91.9 7.9 %collective-permute-start.13 = (bf16[4,2,160,768]{3,2,1,0:T(8,128)(2,1)}, bf16[4,2,160,768]{3,2,1,0:T(8,128)(2,1)S(1)}, u32[]{:S(2)}, u32[]{:S(2)}) collective-permute-start(bf16[4,2,160,768]{3,2,1,0:T(8,128)(2,1)} %hold.3.refs_2_), channel_id=1, source_target_pairs={{0,16},{1,17},{2,18},{3,19},{4,20},{5,21},{6,22},{7,23},{8,24},{9,... | collective-permute-start | bytes 5898248 | tf_op jit(solution)/shard_map/ppermute | solution.py:47
  117.2 9.7 %collective-permute-start.15 = (bf16[8,160,1536]{2,1,0:T(8,128)(2,1)S(1)}, bf16[8,160,1536]{2,1,0:T(8,128)(2,1)S(1)}, u32[]{:S(2)}, u32[]{:S(2)}) collective-permute-start(bf16[8,160,1536]{2,1,0:T(8,128)(2,1)S(1)} %get-tuple-element.85), channel_id=1, source_target_pairs={{0,16},{1,17},{2,18},{3,19},{4,20},{5,21},{6,22},{7,23},{8,24},{9,... | collective-permute-start | bytes 11796488 | tf_op jit(solution)/shard_map/ppermute | solution.py:47
  126.3 4.8 %collective-permute-start.14 = (bf16[8,160,768]{2,1,0:T(8,128)(2,1)S(1)}, bf16[8,160,768]{2,1,0:T(8,128)(2,1)S(1)}, u32[]{:S(2)}, u32[]{:S(2)}) collective-permute-start(bf16[8,160,768]{2,1,0:T(8,128)(2,1)S(1)} %get-tuple-element.84), channel_id=1, source_target_pairs={{0,16},{1,17},{2,18},{3,19},{4,20},{5,21},{6,22},{7,23},{8,24},{9,... | collective-permute-start | bytes 5898248 | tf_op jit(solution)/shard_map/ppermute | solution.py:47
  126.9 6.3 %slice-start = ((s8[7864320]{0:T(1024)(128)(4,1)}), s8[4194304]{0:T(1024)(128)(4,1)S(1)}, s32[]{:S(2)}) async-start(s8[7864320]{0:T(1024)(128)(4,1)} %bitcast.15), calls=%async_computation.2 | async-start | bytes 8388608
  126.9 6.3 %slice-start.1 = ((s8[7864320]{0:T(1024)(128)(4,1)}), s8[3670016]{0:T(1024)(128)(4,1)S(1)}, s32[]{:S(2)}) async-start(s8[7864320]{0:T(1024)(128)(4,1)} %bitcast.15), calls=%async_computation.3 | async-start | bytes 7340032
  128.1 24.3 %collective-permute-start.20 = (bf16[2,160,1536]{2,1,0:T(8,128)(2,1)S(1)}, bf16[2,160,1536]{2,1,0:T(8,128)(2,1)S(1)}, u32[]{:S(2)}, u32[]{:S(2)}) collective-permute-start(bf16[2,160,1536]{2,1,0:T(8,128)(2,1)S(1)} %get-tuple-element.92), channel_id=1, source_target_pairs={{0,96},{1,97},{2,98},{3,99},{4,100},{5,101},{6,102},{7,103},{8,104... | collective-permute-start | bytes 2949128 | tf_op jit(solution)/shard_map/ppermute | solution.py:47
  131.2 24.6 %collective-permute-start.19 = (bf16[2,160,1536]{2,1,0:T(8,128)(2,1)S(1)}, bf16[2,160,1536]{2,1,0:T(8,128)(2,1)S(1)}, u32[]{:S(2)}, u32[]{:S(2)}) collective-permute-start(bf16[2,160,1536]{2,1,0:T(8,128)(2,1)S(1)} %get-tuple-element.86.refs_2_), channel_id=1, source_target_pairs={{0,32},{1,33},{2,34},{3,35},{4,36},{5,37},{6,38},{7,39},{8,40},{9,... | collective-permute-start | bytes 2949128 | tf_op jit(solution)/shard_map/ppermute | solution.py:47
  131.2 1.3 copy-start.5
  132.5 0.8 copy-start.24
  138.7 32.7 %collective-permute-start.16 = (bf16[104,2688]{1,0:T(8,128)(2,1)S(1)}, bf16[104,2688]{1,0:T(8,128)(2,1)S(1)}, u32[]{:S(2)}, u32[]{:S(2)}) collective-permute-start(bf16[104,2688]{1,0:T(8,128)(2,1)S(1)} %get-tuple-element.89), channel_id=1, source_target_pairs={{1,0},{2,1},{3,2},{128,3},{5,4},{6,5},{7,6},{132,7},{9,8},{10,9},{... | collective-permute-start | bytes 1677320 | tf_op jit(solution)/shard_map/ppermute | solution.py:47
  139.5 31.9 %collective-permute-start.17 = (bf16[104,2688]{1,0:T(8,128)(2,1)S(1)}, bf16[104,2688]{1,0:T(8,128)(2,1)S(1)}, u32[]{:S(2)}, u32[]{:S(2)}) collective-permute-start(bf16[104,2688]{1,0:T(8,128)(2,1)S(1)} %get-tuple-element.90), channel_id=1, source_target_pairs={{2,0},{131,1},{128,2},{1,3},{6,4},{135,5},{132,6},{5,7},{10,8},{13... | collective-permute-start | bytes 1677320 | tf_op jit(solution)/shard_map/ppermute | solution.py:47
  140.9 30.5 %collective-permute-start.18 = (bf16[104,2688]{1,0:T(8,128)(2,1)S(1)}, bf16[104,2688]{1,0:T(8,128)(2,1)S(1)}, u32[]{:S(2)}, u32[]{:S(2)}) collective-permute-start(bf16[104,2688]{1,0:T(8,128)(2,1)S(1)} %get-tuple-element.91), channel_id=1, source_target_pairs={{131,0},{0,1},{1,2},{2,3},{135,4},{4,5},{5,6},{6,7},{139,8},{8,9},... | collective-permute-start | bytes 1677320 | tf_op jit(solution)/shard_map/ppermute | solution.py:47
  156.7 12.1 %collective-permute-start.22 = (bf16[160,1536]{1,0:T(8,128)(2,1)S(1)}, bf16[160,1536]{1,0:T(8,128)(2,1)S(1)}, u32[]{:S(2)}, u32[]{:S(2)}) collective-permute-start(bf16[160,1536]{1,0:T(8,128)(2,1)S(1)} %get-tuple-element.94), channel_id=1, source_target_pairs={{0,96},{1,97},{2,98},{3,99},{4,100},{5,101},{6,102},{7,103},{8,104... | collective-permute-start | bytes 1474568 | tf_op jit(solution)/shard_map/ppermute | solution.py:47
  157.0 13.3 %collective-permute-start.21 = (bf16[160,1536]{1,0:T(8,128)(2,1)S(1)}, bf16[160,1536]{1,0:T(8,128)(2,1)S(1)}, u32[]{:S(2)}, u32[]{:S(2)}) collective-permute-start(bf16[160,1536]{1,0:T(8,128)(2,1)S(1)} %get-tuple-element.93.refs_6_), channel_id=1, source_target_pairs={{0,32},{1,33},{2,34},{3,35},{4,36},{5,37},{6,38},{7,39},{8,40},{9,... | collective-permute-start | bytes 1474568 | tf_op jit(solution)/shard_map/ppermute | solution.py:47
  172.8 1.4 copy-start
  174.2 0.8 copy-start.18
  175.0 37.6 %all-to-all-start.1 = ((bf16[4,104,2688]{2,1,0:T(8,128)(2,1)}), bf16[4,104,2688]{2,1,0:T(8,128)(2,1)}, u32[]{:S(2)}, u32[]{:S(2)}) async-start(bf16[4,104,2688]{2,1,0:T(8,128)(2,1)} %copy-done), calls=%async_computation.1 | async-start | bytes 4472832 | tf_op jit(solution)/shard_map/all_to_all | solution.py:615
  179.5 11.4 %collective-permute-start.24 = (bf16[2,160,768]{2,1,0:T(8,128)(2,1)}, bf16[2,160,768]{2,1,0:T(8,128)(2,1)S(1)}, u32[]{:S(2)}, u32[]{:S(2)}) collective-permute-start(bf16[2,160,768]{2,1,0:T(8,128)(2,1)} %copy-done.24), channel_id=1, source_target_pairs={{0,96},{1,97},{2,98},{3,99},{4,100},{5,101},{6,102},{7,103},{8,104... | collective-permute-start | bytes 1474568 | tf_op jit(solution)/shard_map/ppermute | solution.py:47
  179.8 12.3 %collective-permute-start.23 = (bf16[2,160,768]{2,1,0:T(8,128)(2,1)S(1)}, bf16[2,160,768]{2,1,0:T(8,128)(2,1)S(1)}, u32[]{:S(2)}, u32[]{:S(2)}) collective-permute-start(bf16[2,160,768]{2,1,0:T(8,128)(2,1)S(1)} %get-tuple-element.87.refs_4_), channel_id=1, source_target_pairs={{0,32},{1,33},{2,34},{3,35},{4,36},{5,37},{6,38},{7,39},{8,40},{9,... | collective-permute-start | bytes 1474568 | tf_op jit(solution)/shard_map/ppermute | solution.py:47
  181.6 25.2 %collective-permute-start.27 = (bf16[160,1536]{1,0:T(8,128)(2,1)}, bf16[160,1536]{1,0:T(8,128)(2,1)S(1)}, u32[]{:S(2)}, u32[]{:S(2)}) collective-permute-start(bf16[160,1536]{1,0:T(8,128)(2,1)} %copy-done.18), channel_id=1, source_target_pairs={{0,128},{1,129},{2,130},{3,131},{4,132},{5,133},{6,134},{7,135},{8... | collective-permute-start | bytes 1474568 | tf_op jit(solution)/shard_map/ppermute | solution.py:47
  192.2 1.6 copy-start.1
  193.8 1.5 copy-start.6
  195.8 12.5 %copy-start.7 = (bf16[8,160,768]{2,1,0:T(8,128)(2,1)S(1)}, bf16[8,160,768]{2,1,0:T(8,128)(2,1)}, u32[]{:S(2)}) copy-start(bf16[8,160,768]{2,1,0:T(8,128)(2,1)} %copy-done.5) | copy-start | bytes 5898244
  195.8 12.5 %collective-permute-start.26 = (bf16[160,768]{1,0:T(8,128)(2,1)S(1)}, bf16[160,768]{1,0:T(8,128)(2,1)S(1)}, u32[]{:S(2)}, u32[]{:S(2)}) collective-permute-start(bf16[160,768]{1,0:T(8,128)(2,1)S(1)} %get-tuple-element.98), channel_id=1, source_target_pairs={{0,96},{1,97},{2,98},{3,99},{4,100},{5,101},{6,102},{7,103},{8,104... | collective-permute-start | bytes 737288 | tf_op jit(solution)/shard_map/ppermute | solution.py:47
  196.4 11.9 %collective-permute-start.25 = (bf16[160,768]{1,0:T(8,128)(2,1)S(1)}, bf16[160,768]{1,0:T(8,128)(2,1)S(1)}, u32[]{:S(2)}, u32[]{:S(2)}) collective-permute-start(bf16[160,768]{1,0:T(8,128)(2,1)S(1)} %get-tuple-element.97.refs_2_), channel_id=1, source_target_pairs={{0,32},{1,33},{2,34},{3,35},{4,36},{5,37},{6,38},{7,39},{8,40},{9,... | collective-permute-start | bytes 737288 | tf_op jit(solution)/shard_map/ppermute | solution.py:47
  206.8 5.8 %copy-start.21 = (s32[128,3]{0,1:T(4,128)S(1)}, s32[128,3]{0,1:T(4,128)}, u32[]{:S(2)}) copy-start(s32[128,3]{0,1:T(4,128)} %param.8) | copy-start | bytes 4612
  208.3 1.0 copy-start.10
  209.3 3.2 %copy-start.23 = (bf16[128,3]{0,1:T(4,128)(2,1)S(1)}, bf16[128,3]{0,1:T(4,128)(2,1)}, u32[]{:S(2)}) copy-start(bf16[128,3]{0,1:T(4,128)(2,1)} %param.9) | copy-start | bytes 2308
  209.9 11.6 %collective-permute-start.28 = (bf16[160,768]{1,0:T(8,128)(2,1)S(1)}, bf16[160,768]{1,0:T(8,128)(2,1)S(1)}, u32[]{:S(2)}, u32[]{:S(2)}) collective-permute-start(bf16[160,768]{1,0:T(8,128)(2,1)S(1)} %get-tuple-element.100.refs_5_), channel_id=1, source_target_pairs={{0,128},{1,129},{2,130},{3,131},{4,132},{5,133},{6,134},{7,135},{8... | collective-permute-start | bytes 737288 | tf_op jit(solution)/shard_map/ppermute | solution.py:47
  221.5 1.1 copy-start.11

commit v2 on v1

--- a/solution.py
+++ b/solution.py
@@ -291,7 +291,7 @@
         acc[...] = jnp.zeros_like(acc)
 
     c = pos[4]
-    for j in range(2):
+    for j in range(4):
         own = pl.multiple_of((2 * j + c) * part, 32)
         other = pl.multiple_of((2 * j + 1 - c) * part, 32)
         wbuf[pl.ds(own, part), :] = w_own[j, 0]
@@ -314,7 +314,7 @@
     hid = hidden.shape[1]
     part = w_own.shape[2]
     w_spec = pl.BlockSpec(
-        (2, 1, part, hid), lambda b, p: (lax.rem(b, 2), lax.rem(lax.div(b, 2) + p[2], 2), 0, 0)
+        (4, 1, part, hid), lambda b, p: (0, lax.rem(b + p[2], 2), 0, 0)
     )
     anys = pl.BlockSpec(memory_space=pl.ANY)
     whole = lambda *shape: pl.BlockSpec(shape, lambda b, p: (0,) * len(shape))
@@ -327,12 +327,12 @@
         ],
         grid_spec=pltpu.PrefetchScalarGridSpec(
             num_scalar_prefetch=1,
-            grid=(4,),
-            in_specs=[pl.BlockSpec((slots, 4 * part), lambda b, p: (0, b)), w_spec, w_spec]
+            grid=(2,),
+            in_specs=[pl.BlockSpec((slots, 8 * part), lambda b, p: (0, b)), w_spec, w_spec]
             + [anys] * (3 + len(deps)),
             out_specs=[whole(slots, hid), whole(slots, hid), whole(slots, 128)],
             scratch_shapes=[
-                pltpu.VMEM((4 * part, hid), BF),
+                pltpu.VMEM((8 * part, hid), BF),
                 pltpu.VMEM((slots, hid), F32),
                 pltpu.VMEM((slots, hid), BF),
                 pltpu.VMEM((slots, hid), F32),

time: 224 us -> 223 us (level)
  no operation moved by 1% of the time
where the time goes in v2:
time: 223 us; the launch traced here: 222 us
  waiting for transfers between devices  91.8 us (41%)
  Pallas kernels  61 us (27%)
  starting transfers between devices  48.1 us (22%)
  local copies, waits for them, and re-layouts  20.3 us (9%)
    ppermute x29, waiting for transfers between devices, send(): return lax.ppermute(v, AXES, pairs)  91.8 us
    pallas_call x20, Pallas kernels, call(): pl.pallas_call(body, out_shape=out_shape, in_specs=specs, out_specs=out_s...  49.3 us
    ppermute x29, starting transfers between devices, send(): return lax.ppermute(v, AXES, pairs)  39.2 us
    unnamed x54, local copies, waits for them, and re-layouts  20.2 us
    pallas_call x1, Pallas kernels, up_part(): pl.pallas_call(up_kernel, grid=(steps,), out_shape=[jax.ShapeDtypeStruct(...  6.25 us
    pallas_call x1, Pallas kernels, down_part(): pl.pallas_call(functools.partial(down_kernel, part), out_shape=[jax.Shape...  5.48 us
    all_to_all x1, starting transfers between devices, on_device(): back_rows_x = lax.all_to_all(back_rows, 'x', 0, 0, tiled=True)  4.48 us
    all_to_all x1, starting transfers between devices, on_device(): wd_own = lax.all_to_all(pairs, 'y', 0, 0, tiled=True)  4.46 us
  transfers between devices with their start and end apart: 31, of which 15 were waited for; matrix products, arithmetic and copies ran while one was open for 0% of the time, Pallas kernels for 19%

profile of v2, /device:TPU:34, one launch (start us, length us, event | category | flops | bytes accessed | tf_op | source)
XLA Modules:
  0.0 222.2 jit_solution(10299672690927674627)
XLA Ops:
  0.6 6.4 %collective-permute-start = (bf16[160,768]{1,0:T(8,128)(2,1)}, bf16[160,768]{1,0:T(8,128)(2,1)S(1)}, u32[]{:S(2)}, u32[]{:S(2)}) collective-permute-start(bf16[160,768]{1,0:T(8,128)(2,1)} %bitcast.18), channel_id=1, source_target_pairs={{0,128},{1,129},{2,130},{3,131},{4,132},{5,133},{6,134},{7,135},{8... | collective-permute-start | bytes 737288 | tf_op jit(solution)/shard_map/ppermute | solution.py:47
  7.1 1.1 copy-done.12
  8.2 1.1 copy-done.13
  10.7 2.9 %prep.1 = (bf16[104,2560]{1,0:T(8,128)(2,1)S(1)}, bf16[104,2560]{1,0:T(8,128)(2,1)S(1)}, bf16[104,2560]{1,0:T(8,128)(2,1)S(1)}, bf16[104,2560]{1,0:T(8,128)(2,1)...) custom-call(s32[13]{0:T(128)S(1)} %concatenate.3.refs_0_, ...), custom_call_target="tpu_custom_call" | custom-call | flops 8519680 | bytes 87040 | tf_op jit(solution)/shard_map/prep/pallas_call | solution.py:108
  13.6 0.8 copy-done.16
  14.4 4.2 %collective-permute-done.refs_3_.refs_1_ = bf16[160,768]{1,0:T(8,128)(2,1)S(1)} collective-permute-done((bf16[160,768]{1,0:T(8,128)(2,1)}, bf16[160,768]{1,0:T(8,128)(2,1)S(1)}, u32[]{:S(2)}, u32[]{:S(2)}) %collective-permute-start) | collective-permute-done | bytes 245792 | tf_op jit(solution)/shard_map/ppermute | solution.py:47
  18.5 1.4 collective-permute-start.1
  19.9 1.5 collective-permute-start.7
  21.4 1.1 collective-permute-start.2
  22.9 1.1 collective-permute-start.8
  24.0 9.6 %collective-permute-done.1.refs_2_.refs_1_ = bf16[104,2560]{1,0:T(8,128)(2,1)S(1)} collective-permute-done((bf16[104,2560]{1,0:T(8,128)(2,1)S(1)}, bf16[104,2560]{1,0:T(8,128)(2,1)S(1)}, u32[]{:S(2)}, u32[]{:S(2)}) %collective-permute-start.1) | collective-permute-done | bytes 532512 | tf_op jit(solution)/shard_map/ppermute | solution.py:47
  34.1 1.5 pair_parts.1.refs_4_
  35.6 4.5 %all-to-all-start = ((bf16[4,2,160,768]{3,2,1,0:T(8,128)(2,1)}), bf16[4,2,160,768]{3,2,1,0:T(8,128)(2,1)}, u32[]{:S(2)}, u32[]{:S(2)}) async-start(bf16[4,2,160,768]{3,2,1,0:T(8,128)(2,1)} %pair_parts.1.refs_4_), calls=%async_computation | async-start | bytes 3932160 | tf_op jit(solution)/shard_map/all_to_all | solution.py:597
  40.1 6.4 %collective-permute-done.3.refs_3_ = bf16[104,2560]{1,0:T(8,128)(2,1)} collective-permute-done((bf16[104,2560]{1,0:T(8,128)(2,1)}, bf16[104,2560]{1,0:T(8,128)(2,1)}, u32[]{:S(2)}, u32[]{:S(2)}) %collective-permute-start.3) | collective-permute-done | bytes 532512 | tf_op jit(solution)/shard_map/ppermute | solution.py:47
  46.4 1.0 copy-done.17
  47.5 3.3 %regroup.3 = (bf16[104,2560]{1,0:T(8,128)(2,1)S(1)}, bf16[104,2560]{1,0:T(8,128)(2,1)S(1)}, bf16[104,2560]{1,0:T(8,128)(2,1)S(1)}, bf16[104,2560]{1,0:T(8,128)(2,1)S(1)}) custom-call(bf16[104,2560]{1,0:T(8,128)(2,1)S(1)} %copy-done.17, bf16[104,2560]{1,0:T(8,128)(2,1)S(1)} %collective-permute-done.1.refs_2_.refs_1_, ...), custom_call_target="tpu_custom_call" | custom-call | bytes 66560 | tf_op jit(solution)/shard_map/regroup/pallas_call | solution.py:108
  50.8 3.4 %regroup.4 = (bf16[104,2560]{1,0:T(8,128)(2,1)S(1)}, bf16[104,2560]{1,0:T(8,128)(2,1)S(1)}, bf16[104,2560]{1,0:T(8,128)(2,1)S(1)}, bf16[104,2560]{1,0:T(8,128)(2,1)S(1)}) custom-call(bf16[104,2560]{1,0:T(8,128)(2,1)S(1)} %copy-done.15, bf16[104,2560]{1,0:T(8,128)(2,1)} %collective-permute-done.7.refs_1_, bf16[104,2560]{1,0:T(8,128)(2,1)} %collective-permute-done.8.refs_2_, ...), custom_call_target="tpu_custom_call" | custom-call | bytes 66560 | tf_op jit(solution)/shard_map/regroup/pallas_call | solution.py:108
  54.2 1.1 collective-permute-start.10
  55.3 3.5 %collective-permute-start.11 = (bf16[104,2560]{1,0:T(8,128)(2,1)S(1)}, bf16[104,2560]{1,0:T(8,128)(2,1)S(1)}, u32[]{:S(2)}, u32[]{:S(2)}) collective-permute-start(bf16[104,2560]{1,0:T(8,128)(2,1)S(1)} %get-tuple-element.72), channel_id=1, source_target_pairs={{0,2},{1,131},{2,128},{3,1},{4,6},{5,135},{6,132},{7,5},{8,10},{9,... | collective-permute-start | bytes 1597448 | tf_op jit(solution)/shard_map/ppermute | solution.py:47
  59.3 1.2 collective-permute-start.4
  60.5 1.4 collective-permute-start.5
  61.9 7.3 %collective-permute-done.10.refs_5_ = bf16[104,2560]{1,0:T(8,128)(2,1)S(1)} collective-permute-done((bf16[104,2560]{1,0:T(8,128)(2,1)S(1)}, bf16[104,2560]{1,0:T(8,128)(2,1)S(1)}, u32[]{:S(2)}, u32[]{:S(2)}) %collective-permute-start.10) | collective-permute-done | bytes 532512 | tf_op jit(solution)/shard_map/ppermute | solution.py:47
  69.8 1.6 collective-permute-done.11.refs_6_
  71.3 10.2 %collective-permute-done.12.refs_7_ = bf16[104,2560]{1,0:T(8,128)(2,1)S(1)} collective-permute-done((bf16[104,2560]{1,0:T(8,128)(2,1)S(1)}, bf16[104,2560]{1,0:T(8,128)(2,1)S(1)}, u32[]{:S(2)}, u32[]{:S(2)}) %collective-permute-start.12) | collective-permute-done | bytes 532512 | tf_op jit(solution)/shard_map/ppermute | solution.py:47
  81.5 4.8 %collective-permute-done.6.refs_3_ = bf16[104,2560]{1,0:T(8,128)(2,1)S(1)} collective-permute-done((bf16[104,2560]{1,0:T(8,128)(2,1)S(1)}, bf16[104,2560]{1,0:T(8,128)(2,1)S(1)}, u32[]{:S(2)}, u32[]{:S(2)}) %collective-permute-start.6) | collective-permute-done | bytes 532512 | tf_op jit(solution)/shard_map/ppermute | solution.py:47
  86.3 1.2 assemble.1
  87.5 1.4 copy-done.2
  88.9 1.3 copy-done.8
  90.3 1.6 copy-done.3
  91.9 1.6 copy-done.4
  93.5 6.3 %up_part.1 = (bf16[416,768]{1,0:T(8,128)(2,1)S(1)}, f32[416,768]{1,0:T(8,128)S(1)}, f32[416,768]{1,0:T(8,128)S(1)}) custom-call(bf16[416,2560]{1,0:T(8,128)(2,1)S(1)} %copy-done.4, bf16[1,2560,1536]{2,1,0:T(8,128)(2,1)} %refs_2_.1, bf16[1,2560,1536]{2,1,0:T(8,128)(2,1)} %refs_2_.1), custom_call_target="tpu_custom_call" | custom-call | flops 51118080 | bytes 156160 | tf_op jit(solution)/shard_map/up_part/pallas_call | solution.py:258
  99.7 5.5 %down_part.1 = (bf16[416,768]{1,0:T(8,128)(2,1)S(1)}, bf16[416,768]{1,0:T(8,128)(2,1)S(1)}, f32[416,128]{1,0:T(8,128)S(1)}) custom-call(s32[13]{0:T(128)S(1)} %concatenate.3.refs_0_, bf16[416,2560]{1,0:T(8,128)(2,1)S(1)} %copy-done.9, bf16[4,2,160,768]{3,2,1,0:T(8,128)(2,1)} %hold.3.refs_2_, bf16[4,2,160,768]{3,2,1,0:T(8,128)(2,1)S(1)} %collective-permute-done.13.refs_3_, ...), custom_call_target="tpu_custom_call" | custom-call | flops 25559040 | bytes 94720 | tf_op jit(solution)/shard_map/down_part/pallas_call | solution.py:321
  105.2 10.9 %grad_part.2 = (bf16[8,160,1536]{2,1,0:T(8,128)(2,1)S(1)}, bf16[8,160,1536]{2,1,0:T(8,128)(2,1)S(1)}) custom-call(s32[13]{0:T(128)S(1)} %concatenate.3.refs_0_, bf16[416,2560]{1,0:T(8,128)(2,1)S(1)} %copy-done.4, bf16[416,768]{1,0:T(8,128)(2,1)S(1)} %get-tuple-element.79.refs_2_.refs_0_, bf16[416,768]{1,0:T(8,128)(2,1)S(1)} %get-tuple-element.80.refs_3_.refs_1_), custom_call_target="tpu_custom_call" | custom-call | flops 51118080 | bytes 156160 | tf_op jit(solution)/shard_map/grad_part/pallas_call | solution.py:108
  116.2 9.0 %grad_part.3 = (bf16[8,160,768]{2,1,0:T(8,128)(2,1)S(1)}, bf16[8,160,768]{2,1,0:T(8,128)(2,1)S(1)}) custom-call(s32[13]{0:T(128)S(1)} %concatenate.3.refs_0_, bf16[416,2560]{1,0:T(8,128)(2,1)S(1)} %copy-done.9, bf16[416,768]{1,0:T(8,128)(2,1)S(1)} %get-tuple-element.76.refs_4_.refs_2_, bf16[8,160,1536]{2,1,0:T(8,128)(2,1)S(1)} %get-tuple-element.82.refs_3_.refs_0_), custom_call_target="tpu_custom_call" | custom-call | flops 25559040 | bytes 94720 | tf_op jit(solution)/shard_map/grad_part/pallas_call | solution.py:108
  125.8 1.1 first_sum.2
  126.9 3.1 %collective-permute-start.20 = (bf16[2,160,1536]{2,1,0:T(8,128)(2,1)S(1)}, bf16[2,160,1536]{2,1,0:T(8,128)(2,1)S(1)}, u32[]{:S(2)}, u32[]{:S(2)}) collective-permute-start(bf16[2,160,1536]{2,1,0:T(8,128)(2,1)S(1)} %get-tuple-element.92), channel_id=1, source_target_pairs={{0,96},{1,97},{2,98},{3,99},{4,100},{5,101},{6,102},{7,103},{8,104... | collective-permute-start | bytes 2949128 | tf_op jit(solution)/shard_map/ppermute | solution.py:47
  132.1 5.5 %row_part.1 = (bf16[104,2688]{1,0:T(8,128)(2,1)S(1)}, bf16[104,2688]{1,0:T(8,128)(2,1)S(1)}, bf16[104,2688]{1,0:T(8,128)(2,1)S(1)}, bf16[104,2688]{1,0:T(8,128)(2,1)S(1)}) custom-call(bf16[416,768]{1,0:T(8,128)(2,1)S(1)} %get-tuple-element.79.refs_2_.refs_0_, bf16[416,768]{1,0:T(8,128)(2,1)S(1)} %get-tuple-element.80.refs_3_.refs_1_, ...), custom_call_target="tpu_custom_call" | custom-call | flops 51118080 | bytes 152832 | tf_op jit(solution)/shard_map/row_part/pallas_call | solution.py:108
  138.4 1.4 collective-permute-start.17
  139.8 1.1 collective-permute-start.18
  140.8 10.4 %collective-permute-done.20.refs_3_ = bf16[2,160,1536]{2,1,0:T(8,128)(2,1)S(1)} collective-permute-done((bf16[2,160,1536]{2,1,0:T(8,128)(2,1)S(1)}, bf16[2,160,1536]{2,1,0:T(8,128)(2,1)S(1)}, u32[]{:S(2)}, u32[]{:S(2)}) %collective-permute-start.20) | collective-permute-done | bytes 983072 | tf_op jit(solution)/shard_map/ppermute | solution.py:47
  151.3 3.4 %collective-permute-done.19.refs_2_ = bf16[2,160,1536]{2,1,0:T(8,128)(2,1)S(1)} collective-permute-done((bf16[2,160,1536]{2,1,0:T(8,128)(2,1)S(1)}, bf16[2,160,1536]{2,1,0:T(8,128)(2,1)S(1)}, u32[]{:S(2)}, u32[]{:S(2)}) %collective-permute-start.19) | collective-permute-done | bytes 983072 | tf_op jit(solution)/shard_map/ppermute | solution.py:47
  154.7 0.9 second_sum.2
  155.9 1.7 collective-permute-start.21
  157.6 10.0 %collective-permute-done.22.refs_5_ = bf16[160,1536]{1,0:T(8,128)(2,1)S(1)} collective-permute-done((bf16[160,1536]{1,0:T(8,128)(2,1)S(1)}, bf16[160,1536]{1,0:T(8,128)(2,1)S(1)}, u32[]{:S(2)}, u32[]{:S(2)}) %collective-permute-start.22) | collective-permute-done | bytes 491552 | tf_op jit(solution)/shard_map/ppermute | solution.py:47
  167.6 1.5 collective-permute-done.21.refs_4_
  169.2 1.1 far_sum.2
  170.3 1.3 regroup.5.refs_4_
  171.6 1.4 copy-done
  173.8 4.5 %all-to-all-start.1 = ((bf16[4,104,2688]{2,1,0:T(8,128)(2,1)}), bf16[4,104,2688]{2,1,0:T(8,128)(2,1)}, u32[]{:S(2)}, u32[]{:S(2)}) async-start(bf16[4,104,2688]{2,1,0:T(8,128)(2,1)} %copy-done), calls=%async_computation.1 | async-start | bytes 4472832 | tf_op jit(solution)/shard_map/all_to_all | solution.py:615
  178.7 1.7 collective-permute-start.23
  180.4 2.6 %collective-permute-start.27 = (bf16[160,1536]{1,0:T(8,128)(2,1)}, bf16[160,1536]{1,0:T(8,128)(2,1)S(1)}, u32[]{:S(2)}, u32[]{:S(2)}) collective-permute-start(bf16[160,1536]{1,0:T(8,128)(2,1)} %copy-done.18), channel_id=1, source_target_pairs={{0,128},{1,129},{2,130},{3,131},{4,132},{5,133},{6,134},{7,135},{8... | collective-permute-start | bytes 1474568 | tf_op jit(solution)/shard_map/ppermute | solution.py:47
  183.0 6.7 %collective-permute-done.24.refs_3_ = bf16[2,160,768]{2,1,0:T(8,128)(2,1)S(1)} collective-permute-done((bf16[2,160,768]{2,1,0:T(8,128)(2,1)}, bf16[2,160,768]{2,1,0:T(8,128)(2,1)S(1)}, u32[]{:S(2)}, u32[]{:S(2)}) %collective-permute-start.24) | collective-permute-done | bytes 491552 | tf_op jit(solution)/shard_map/ppermute | solution.py:47
  189.7 1.3 collective-permute-done.23.refs_2_
  191.0 1.6 copy-done.1
  192.7 1.5 copy-done.6
  195.2 1.5 collective-permute-start.25
  196.8 8.9 %collective-permute-done.27.refs_1_ = bf16[160,1536]{1,0:T(8,128)(2,1)S(1)} collective-permute-done((bf16[160,1536]{1,0:T(8,128)(2,1)}, bf16[160,1536]{1,0:T(8,128)(2,1)S(1)}, u32[]{:S(2)}, u32[]{:S(2)}) %collective-permute-start.27) | collective-permute-done | bytes 491552 | tf_op jit(solution)/shard_map/ppermute | solution.py:47
  205.6 1.5 last_sum.2.refs_6_
  207.1 1.0 copy-done.10
  208.7 2.7 %collective-permute-start.28 = (bf16[160,768]{1,0:T(8,128)(2,1)S(1)}, bf16[160,768]{1,0:T(8,128)(2,1)S(1)}, u32[]{:S(2)}, u32[]{:S(2)}) collective-permute-start(bf16[160,768]{1,0:T(8,128)(2,1)S(1)} %get-tuple-element.100.refs_5_), channel_id=1, source_target_pairs={{0,128},{1,129},{2,130},{3,131},{4,132},{5,133},{6,134},{7,135},{8... | collective-permute-start | bytes 737288 | tf_op jit(solution)/shard_map/ppermute | solution.py:47
  211.4 3.3 %final.1 = (bf16[128,2560]{1,0:T(8,128)(2,1)}, bf16[3,128]{1,0:T(4,128)(2,1)}) custom-call(s32[13]{0:T(128)S(1)} %concatenate.3.refs_0_, s32[3,128]{1,0:T(4,128)S(1)} %bitcast.21, bf16[3,128]{1,0:T(4,128)(2,1)S(1)} %bitcast.23, bf16[416,128]{1,0:T(8,128)(2,1)S(1)} %get-tuple-element.54.refs_3_, bf16[4,104,2688]{2,1,0:T(8,128)(2,1)} %all-to-all-done.1.refs_4_, ...), custom_call_target="tpu_custom_call" | custom-call | flops 4259840 | bytes 43520 | tf_op jit(solution)/shard_map/final/pallas_call | solution.py:108
  214.8 5.6 %collective-permute-done.28.refs_1_ = bf16[160,768]{1,0:T(8,128)(2,1)S(1)} collective-permute-done((bf16[160,768]{1,0:T(8,128)(2,1)S(1)}, bf16[160,768]{1,0:T(8,128)(2,1)S(1)}, u32[]{:S(2)}, u32[]{:S(2)}) %collective-permute-start.28) | collective-permute-done | bytes 245792 | tf_op jit(solution)/shard_map/ppermute | solution.py:47
  220.3 1.1 copy-done.11
  221.4 0.8 last_sum.3
  (77 shorter events, 10.1 us)
Async XLA Ops:
  0.6 17.9 %collective-permute-start = (bf16[160,768]{1,0:T(8,128)(2,1)}, bf16[160,768]{1,0:T(8,128)(2,1)S(1)}, u32[]{:S(2)}, u32[]{:S(2)}) collective-permute-start(bf16[160,768]{1,0:T(8,128)(2,1)} %bitcast.18), channel_id=1, source_target_pairs={{0,128},{1,129},{2,130},{3,131},{4,132},{5,133},{6,134},{7,135},{8... | collective-permute-start | bytes 737288 | tf_op jit(solution)/shard_map/ppermute | solution.py:47
  7.1 1.1 copy-start.12
  8.2 1.1 copy-start.13
  9.3 0.7 copy-start.20
  10.0 0.7 copy-start.22
  10.7 23.5 %copy-start.19 = (bf16[1,768,160]{1,2,0:T(8,128)(2,1)S(1)}, bf16[1,768,160]{1,2,0:T(8,128)(2,1)}, u32[]{:S(2)}) copy-start(bf16[1,768,160]{1,2,0:T(8,128)(2,1)} %param.11) | copy-start | bytes 737284
  13.6 0.8 copy-start.16
  14.4 19.2 %copy-start.14 = (bf16[104,2560]{1,0:T(8,128)(2,1)}, bf16[104,2560]{1,0:T(8,128)(2,1)S(1)}, u32[]{:S(2)}) copy-start(bf16[104,2560]{1,0:T(8,128)(2,1)S(1)} %get-tuple-element.66.refs_0_) | copy-start | bytes 1597444
  18.5 15.0 %collective-permute-start.1 = (bf16[104,2560]{1,0:T(8,128)(2,1)S(1)}, bf16[104,2560]{1,0:T(8,128)(2,1)S(1)}, u32[]{:S(2)}, u32[]{:S(2)}) collective-permute-start(bf16[104,2560]{1,0:T(8,128)(2,1)S(1)} %get-tuple-element.59), channel_id=1, source_target_pairs={{0,1},{1,2},{2,3},{3,128},{4,5},{5,6},{6,7},{7,132},{8,9},{9,10},{... | collective-permute-start | bytes 1597448 | tf_op jit(solution)/shard_map/ppermute | solution.py:47
  19.9 30.9 %collective-permute-start.7 = (bf16[104,2560]{1,0:T(8,128)(2,1)}, bf16[104,2560]{1,0:T(8,128)(2,1)}, u32[]{:S(2)}, u32[]{:S(2)}) collective-permute-start(bf16[104,2560]{1,0:T(8,128)(2,1)} %get-tuple-element.67), channel_id=1, source_target_pairs={{0,4},{1,5},{2,6},{3,7},{4,8},{5,9},{6,10},{7,11},{8,12},{9,13},{1... | collective-permute-start | bytes 1597448 | tf_op jit(solution)/shard_map/ppermute | solution.py:47
  21.4 18.7 %collective-permute-start.2 = (bf16[104,2560]{1,0:T(8,128)(2,1)S(1)}, bf16[104,2560]{1,0:T(8,128)(2,1)}, u32[]{:S(2)}, u32[]{:S(2)}) collective-permute-start(bf16[104,2560]{1,0:T(8,128)(2,1)S(1)} %get-tuple-element.60), channel_id=1, source_target_pairs={{0,2},{1,131},{2,128},{3,1},{4,6},{5,135},{6,132},{7,5},{8,10},{9,... | collective-permute-start | bytes 1597448 | tf_op jit(solution)/shard_map/ppermute | solution.py:47
  22.5 24.0 %collective-permute-start.3 = (bf16[104,2560]{1,0:T(8,128)(2,1)}, bf16[104,2560]{1,0:T(8,128)(2,1)}, u32[]{:S(2)}, u32[]{:S(2)}) collective-permute-start(bf16[104,2560]{1,0:T(8,128)(2,1)} %get-tuple-element.61), channel_id=1, source_target_pairs={{0,131},{1,0},{2,1},{3,2},{4,135},{5,4},{6,5},{7,6},{8,139},{9,8},... | collective-permute-start | bytes 1597448 | tf_op jit(solution)/shard_map/ppermute | solution.py:47
  22.9 27.9 %collective-permute-start.8 = (bf16[104,2560]{1,0:T(8,128)(2,1)S(1)}, bf16[104,2560]{1,0:T(8,128)(2,1)}, u32[]{:S(2)}, u32[]{:S(2)}) collective-permute-start(bf16[104,2560]{1,0:T(8,128)(2,1)S(1)} %get-tuple-element.68), channel_id=1, source_target_pairs={{0,8},{1,9},{2,10},{3,11},{4,12},{5,13},{6,14},{7,15},{8,0},{9,1},... | collective-permute-start | bytes 1597448 | tf_op jit(solution)/shard_map/ppermute | solution.py:47
  33.6 17.2 %collective-permute-start.9 = (bf16[104,2560]{1,0:T(8,128)(2,1)S(1)}, bf16[104,2560]{1,0:T(8,128)(2,1)}, u32[]{:S(2)}, u32[]{:S(2)}) collective-permute-start(bf16[104,2560]{1,0:T(8,128)(2,1)S(1)} %get-tuple-element.69), channel_id=1, source_target_pairs={{0,12},{1,13},{2,14},{3,15},{4,0},{5,1},{6,2},{7,3},{8,4},{9,5},{1... | collective-permute-start | bytes 1597448 | tf_op jit(solution)/shard_map/ppermute | solution.py:47
  35.6 54.7 %all-to-all-start = ((bf16[4,2,160,768]{3,2,1,0:T(8,128)(2,1)}), bf16[4,2,160,768]{3,2,1,0:T(8,128)(2,1)}, u32[]{:S(2)}, u32[]{:S(2)}) async-start(bf16[4,2,160,768]{3,2,1,0:T(8,128)(2,1)} %pair_parts.1.refs_4_), calls=%async_computation | async-start | bytes 3932160 | tf_op jit(solution)/shard_map/all_to_all | solution.py:597
  46.4 1.0 copy-start.17
  47.5 3.3 %copy-start.15 = (bf16[104,2560]{1,0:T(8,128)(2,1)S(1)}, bf16[104,2560]{1,0:T(8,128)(2,1)}, u32[]{:S(2)}) copy-start(bf16[104,2560]{1,0:T(8,128)(2,1)} %copy-done.14) | copy-start | bytes 1597444
  54.2 15.0 %collective-permute-start.10 = (bf16[104,2560]{1,0:T(8,128)(2,1)S(1)}, bf16[104,2560]{1,0:T(8,128)(2,1)S(1)}, u32[]{:S(2)}, u32[]{:S(2)}) collective-permute-start(bf16[104,2560]{1,0:T(8,128)(2,1)S(1)} %get-tuple-element.71), channel_id=1, source_target_pairs={{0,1},{1,2},{2,3},{3,128},{4,5},{5,6},{6,7},{7,132},{8,9},{9,10},{... | collective-permute-start | bytes 1597448 | tf_op jit(solution)/shard_map/ppermute | solution.py:47
  55.3 16.0 %collective-permute-start.11 = (bf16[104,2560]{1,0:T(8,128)(2,1)S(1)}, bf16[104,2560]{1,0:T(8,128)(2,1)S(1)}, u32[]{:S(2)}, u32[]{:S(2)}) collective-permute-start(bf16[104,2560]{1,0:T(8,128)(2,1)S(1)} %get-tuple-element.72), channel_id=1, source_target_pairs={{0,2},{1,131},{2,128},{3,1},{4,6},{5,135},{6,132},{7,5},{8,10},{9,... | collective-permute-start | bytes 1597448 | tf_op jit(solution)/shard_map/ppermute | solution.py:47
  58.8 22.7 %collective-permute-start.12 = (bf16[104,2560]{1,0:T(8,128)(2,1)S(1)}, bf16[104,2560]{1,0:T(8,128)(2,1)S(1)}, u32[]{:S(2)}, u32[]{:S(2)}) collective-permute-start(bf16[104,2560]{1,0:T(8,128)(2,1)S(1)} %get-tuple-element.73), channel_id=1, source_target_pairs={{0,131},{1,0},{2,1},{3,2},{4,135},{5,4},{6,5},{7,6},{8,139},{9,8},... | collective-permute-start | bytes 1597448 | tf_op jit(solution)/shard_map/ppermute | solution.py:47
  59.3 22.2 %collective-permute-start.4 = (bf16[104,2560]{1,0:T(8,128)(2,1)S(1)}, bf16[104,2560]{1,0:T(8,128)(2,1)S(1)}, u32[]{:S(2)}, u32[]{:S(2)}) collective-permute-start(bf16[104,2560]{1,0:T(8,128)(2,1)S(1)} %get-tuple-element.63), channel_id=1, source_target_pairs={{0,4},{1,5},{2,6},{3,7},{4,8},{5,9},{6,10},{7,11},{8,12},{9,13},{1... | collective-permute-start | bytes 1597448 | tf_op jit(solution)/shard_map/ppermute | solution.py:47
  60.5 21.0 %collective-permute-start.5 = (bf16[104,2560]{1,0:T(8,128)(2,1)S(1)}, bf16[104,2560]{1,0:T(8,128)(2,1)S(1)}, u32[]{:S(2)}, u32[]{:S(2)}) collective-permute-start(bf16[104,2560]{1,0:T(8,128)(2,1)S(1)} %get-tuple-element.64), channel_id=1, source_target_pairs={{0,8},{1,9},{2,10},{3,11},{4,12},{5,13},{6,14},{7,15},{8,0},{9,1},... | collective-permute-start | bytes 1597448 | tf_op jit(solution)/shard_map/ppermute | solution.py:47
  69.2 17.1 %collective-permute-start.6 = (bf16[104,2560]{1,0:T(8,128)(2,1)S(1)}, bf16[104,2560]{1,0:T(8,128)(2,1)S(1)}, u32[]{:S(2)}, u32[]{:S(2)}) collective-permute-start(bf16[104,2560]{1,0:T(8,128)(2,1)S(1)} %get-tuple-element.65), channel_id=1, source_target_pairs={{0,12},{1,13},{2,14},{3,15},{4,0},{5,1},{6,2},{7,3},{8,4},{9,5},{1... | collective-permute-start | bytes 1597448 | tf_op jit(solution)/shard_map/ppermute | solution.py:47
  87.5 1.4 copy-start.2
  88.9 1.3 copy-start.8
  90.2 1.6 copy-start.3
  91.9 1.6 copy-start.4
  91.9 7.9 %copy-start.9 = (bf16[416,2560]{1,0:T(8,128)(2,1)S(1)}, bf16[416,2560]{1,0:T(8,128)(2,1)}, u32[]{:S(2)}) copy-start(bf16[416,2560]{1,0:T(8,128)(2,1)} %copy-done.8) | copy-start | bytes 6389764
  91.9 7.9 %collective-permute-start.13 = (bf16[4,2,160,768]{3,2,1,0:T(8,128)(2,1)}, bf16[4,2,160,768]{3,2,1,0:T(8,128)(2,1)S(1)}, u32[]{:S(2)}, u32[]{:S(2)}) collective-permute-start(bf16[4,2,160,768]{3,2,1,0:T(8,128)(2,1)} %hold.3.refs_2_), channel_id=1, source_target_pairs={{0,16},{1,17},{2,18},{3,19},{4,20},{5,21},{6,22},{7,23},{8,24},{9,... | collective-permute-start | bytes 5898248 | tf_op jit(solution)/shard_map/ppermute | solution.py:47
  116.1 9.7 %collective-permute-start.15 = (bf16[8,160,1536]{2,1,0:T(8,128)(2,1)S(1)}, bf16[8,160,1536]{2,1,0:T(8,128)(2,1)S(1)}, u32[]{:S(2)}, u32[]{:S(2)}) collective-permute-start(bf16[8,160,1536]{2,1,0:T(8,128)(2,1)S(1)} %get-tuple-element.85), channel_id=1, source_target_pairs={{0,16},{1,17},{2,18},{3,19},{4,20},{5,21},{6,22},{7,23},{8,24},{9,... | collective-permute-start | bytes 11796488 | tf_op jit(solution)/shard_map/ppermute | solution.py:47
  125.2 4.8 %collective-permute-start.14 = (bf16[8,160,768]{2,1,0:T(8,128)(2,1)S(1)}, bf16[8,160,768]{2,1,0:T(8,128)(2,1)S(1)}, u32[]{:S(2)}, u32[]{:S(2)}) collective-permute-start(bf16[8,160,768]{2,1,0:T(8,128)(2,1)S(1)} %get-tuple-element.84), channel_id=1, source_target_pairs={{0,16},{1,17},{2,18},{3,19},{4,20},{5,21},{6,22},{7,23},{8,24},{9,... | collective-permute-start | bytes 5898248 | tf_op jit(solution)/shard_map/ppermute | solution.py:47
  125.8 6.3 %slice-start = ((s8[7864320]{0:T(1024)(128)(4,1)}), s8[4194304]{0:T(1024)(128)(4,1)S(1)}, s32[]{:S(2)}) async-start(s8[7864320]{0:T(1024)(128)(4,1)} %bitcast.15), calls=%async_computation.2 | async-start | bytes 8388608
  125.8 6.3 %slice-start.1 = ((s8[7864320]{0:T(1024)(128)(4,1)}), s8[3670016]{0:T(1024)(128)(4,1)S(1)}, s32[]{:S(2)}) async-start(s8[7864320]{0:T(1024)(128)(4,1)} %bitcast.15), calls=%async_computation.3 | async-start | bytes 7340032
  126.9 24.3 %collective-permute-start.20 = (bf16[2,160,1536]{2,1,0:T(8,128)(2,1)S(1)}, bf16[2,160,1536]{2,1,0:T(8,128)(2,1)S(1)}, u32[]{:S(2)}, u32[]{:S(2)}) collective-permute-start(bf16[2,160,1536]{2,1,0:T(8,128)(2,1)S(1)} %get-tuple-element.92), channel_id=1, source_target_pairs={{0,96},{1,97},{2,98},{3,99},{4,100},{5,101},{6,102},{7,103},{8,104... | collective-permute-start | bytes 2949128 | tf_op jit(solution)/shard_map/ppermute | solution.py:47
  130.0 24.6 %collective-permute-start.19 = (bf16[2,160,1536]{2,1,0:T(8,128)(2,1)S(1)}, bf16[2,160,1536]{2,1,0:T(8,128)(2,1)S(1)}, u32[]{:S(2)}, u32[]{:S(2)}) collective-permute-start(bf16[2,160,1536]{2,1,0:T(8,128)(2,1)S(1)} %get-tuple-element.86.refs_2_), channel_id=1, source_target_pairs={{0,32},{1,33},{2,34},{3,35},{4,36},{5,37},{6,38},{7,39},{8,40},{9,... | collective-permute-start | bytes 2949128 | tf_op jit(solution)/shard_map/ppermute | solution.py:47
  130.0 1.3 copy-start.5
  131.3 0.8 copy-start.24
  137.6 32.7 %collective-permute-start.16 = (bf16[104,2688]{1,0:T(8,128)(2,1)S(1)}, bf16[104,2688]{1,0:T(8,128)(2,1)S(1)}, u32[]{:S(2)}, u32[]{:S(2)}) collective-permute-start(bf16[104,2688]{1,0:T(8,128)(2,1)S(1)} %get-tuple-element.89), channel_id=1, source_target_pairs={{1,0},{2,1},{3,2},{128,3},{5,4},{6,5},{7,6},{132,7},{9,8},{10,9},{... | collective-permute-start | bytes 1677320 | tf_op jit(solution)/shard_map/ppermute | solution.py:47
  138.4 31.9 %collective-permute-start.17 = (bf16[104,2688]{1,0:T(8,128)(2,1)S(1)}, bf16[104,2688]{1,0:T(8,128)(2,1)S(1)}, u32[]{:S(2)}, u32[]{:S(2)}) collective-permute-start(bf16[104,2688]{1,0:T(8,128)(2,1)S(1)} %get-tuple-element.90), channel_id=1, source_target_pairs={{2,0},{131,1},{128,2},{1,3},{6,4},{135,5},{132,6},{5,7},{10,8},{13... | collective-permute-start | bytes 1677320 | tf_op jit(solution)/shard_map/ppermute | solution.py:47
  139.8 30.5 %collective-permute-start.18 = (bf16[104,2688]{1,0:T(8,128)(2,1)S(1)}, bf16[104,2688]{1,0:T(8,128)(2,1)S(1)}, u32[]{:S(2)}, u32[]{:S(2)}) collective-permute-start(bf16[104,2688]{1,0:T(8,128)(2,1)S(1)} %get-tuple-element.91), channel_id=1, source_target_pairs={{131,0},{0,1},{1,2},{2,3},{135,4},{4,5},{5,6},{6,7},{139,8},{8,9},... | collective-permute-start | bytes 1677320 | tf_op jit(solution)/shard_map/ppermute | solution.py:47
  155.5 12.1 %collective-permute-start.22 = (bf16[160,1536]{1,0:T(8,128)(2,1)S(1)}, bf16[160,1536]{1,0:T(8,128)(2,1)S(1)}, u32[]{:S(2)}, u32[]{:S(2)}) collective-permute-start(bf16[160,1536]{1,0:T(8,128)(2,1)S(1)} %get-tuple-element.94), channel_id=1, source_target_pairs={{0,96},{1,97},{2,98},{3,99},{4,100},{5,101},{6,102},{7,103},{8,104... | collective-permute-start | bytes 1474568 | tf_op jit(solution)/shard_map/ppermute | solution.py:47
  155.9 13.3 %collective-permute-start.21 = (bf16[160,1536]{1,0:T(8,128)(2,1)S(1)}, bf16[160,1536]{1,0:T(8,128)(2,1)S(1)}, u32[]{:S(2)}, u32[]{:S(2)}) collective-permute-start(bf16[160,1536]{1,0:T(8,128)(2,1)S(1)} %get-tuple-element.93.refs_6_), channel_id=1, source_target_pairs={{0,32},{1,33},{2,34},{3,35},{4,36},{5,37},{6,38},{7,39},{8,40},{9,... | collective-permute-start | bytes 1474568 | tf_op jit(solution)/shard_map/ppermute | solution.py:47
  171.6 1.4 copy-start
  173.0 0.8 copy-start.18
  173.8 37.6 %all-to-all-start.1 = ((bf16[4,104,2688]{2,1,0:T(8,128)(2,1)}), bf16[4,104,2688]{2,1,0:T(8,128)(2,1)}, u32[]{:S(2)}, u32[]{:S(2)}) async-start(bf16[4,104,2688]{2,1,0:T(8,128)(2,1)} %copy-done), calls=%async_computation.1 | async-start | bytes 4472832 | tf_op jit(solution)/shard_map/all_to_all | solution.py:615
  178.3 11.4 %collective-permute-start.24 = (bf16[2,160,768]{2,1,0:T(8,128)(2,1)}, bf16[2,160,768]{2,1,0:T(8,128)(2,1)S(1)}, u32[]{:S(2)}, u32[]{:S(2)}) collective-permute-start(bf16[2,160,768]{2,1,0:T(8,128)(2,1)} %copy-done.24), channel_id=1, source_target_pairs={{0,96},{1,97},{2,98},{3,99},{4,100},{5,101},{6,102},{7,103},{8,104... | collective-permute-start | bytes 1474568 | tf_op jit(solution)/shard_map/ppermute | solution.py:47
  178.7 12.3 %collective-permute-start.23 = (bf16[2,160,768]{2,1,0:T(8,128)(2,1)S(1)}, bf16[2,160,768]{2,1,0:T(8,128)(2,1)S(1)}, u32[]{:S(2)}, u32[]{:S(2)}) collective-permute-start(bf16[2,160,768]{2,1,0:T(8,128)(2,1)S(1)} %get-tuple-element.87.refs_4_), channel_id=1, source_target_pairs={{0,32},{1,33},{2,34},{3,35},{4,36},{5,37},{6,38},{7,39},{8,40},{9,... | collective-permute-start | bytes 1474568 | tf_op jit(solution)/shard_map/ppermute | solution.py:47
  180.4 25.2 %collective-permute-start.27 = (bf16[160,1536]{1,0:T(8,128)(2,1)}, bf16[160,1536]{1,0:T(8,128)(2,1)S(1)}, u32[]{:S(2)}, u32[]{:S(2)}) collective-permute-start(bf16[160,1536]{1,0:T(8,128)(2,1)} %copy-done.18), channel_id=1, source_target_pairs={{0,128},{1,129},{2,130},{3,131},{4,132},{5,133},{6,134},{7,135},{8... | collective-permute-start | bytes 1474568 | tf_op jit(solution)/shard_map/ppermute | solution.py:47
  191.0 1.6 copy-start.1
  192.7 1.5 copy-start.6
  194.6 12.5 %copy-start.7 = (bf16[8,160,768]{2,1,0:T(8,128)(2,1)S(1)}, bf16[8,160,768]{2,1,0:T(8,128)(2,1)}, u32[]{:S(2)}) copy-start(bf16[8,160,768]{2,1,0:T(8,128)(2,1)} %copy-done.5) | copy-start | bytes 5898244
  194.7 12.5 %collective-permute-start.26 = (bf16[160,768]{1,0:T(8,128)(2,1)S(1)}, bf16[160,768]{1,0:T(8,128)(2,1)S(1)}, u32[]{:S(2)}, u32[]{:S(2)}) collective-permute-start(bf16[160,768]{1,0:T(8,128)(2,1)S(1)} %get-tuple-element.98), channel_id=1, source_target_pairs={{0,96},{1,97},{2,98},{3,99},{4,100},{5,101},{6,102},{7,103},{8,104... | collective-permute-start | bytes 737288 | tf_op jit(solution)/shard_map/ppermute | solution.py:47
  195.2 11.9 %collective-permute-start.25 = (bf16[160,768]{1,0:T(8,128)(2,1)S(1)}, bf16[160,768]{1,0:T(8,128)(2,1)S(1)}, u32[]{:S(2)}, u32[]{:S(2)}) collective-permute-start(bf16[160,768]{1,0:T(8,128)(2,1)S(1)} %get-tuple-element.97.refs_2_), channel_id=1, source_target_pairs={{0,32},{1,33},{2,34},{3,35},{4,36},{5,37},{6,38},{7,39},{8,40},{9,... | collective-permute-start | bytes 737288 | tf_op jit(solution)/shard_map/ppermute | solution.py:47
  205.6 5.8 %copy-start.21 = (s32[128,3]{0,1:T(4,128)S(1)}, s32[128,3]{0,1:T(4,128)}, u32[]{:S(2)}) copy-start(s32[128,3]{0,1:T(4,128)} %param.8) | copy-start | bytes 4612
  207.1 1.0 copy-start.10
  208.2 3.3 %copy-start.23 = (bf16[128,3]{0,1:T(4,128)(2,1)S(1)}, bf16[128,3]{0,1:T(4,128)(2,1)}, u32[]{:S(2)}) copy-start(bf16[128,3]{0,1:T(4,128)(2,1)} %param.9) | copy-start | bytes 2308
  208.7 11.6 %collective-permute-start.28 = (bf16[160,768]{1,0:T(8,128)(2,1)S(1)}, bf16[160,768]{1,0:T(8,128)(2,1)S(1)}, u32[]{:S(2)}, u32[]{:S(2)}) collective-permute-start(bf16[160,768]{1,0:T(8,128)(2,1)S(1)} %get-tuple-element.100.refs_5_), channel_id=1, source_target_pairs={{0,128},{1,129},{2,130},{3,131},{4,132},{5,133},{6,134},{7,135},{8... | collective-permute-start | bytes 737288 | tf_op jit(solution)/shard_map/ppermute | solution.py:47
  220.3 1.1 copy-start.11
